TPU v7x, 32 devices: a whole 2x2x4 slice. The times are simulated.
32 devices in a mesh: dp: 8 (over y, x, core), tensor: 4 (over z).
Axes of the slice: x: 2, y: 2, z: 4, core: 2. Of those that a mesh axis runs over, the one named last changes fastest.
Arguments:
- inputs: bfloat16 [8, 1024, 768], P('dp'), may hold values from -8 to 8
- doc_ids: int32 [8, 8], P('dp'), may hold values from 0 to 3, never falling along the last dimension, each value on 1 to 4 neighbouring positions
- qkv_weight: bfloat16 [2, 3, 768, 768], P(None, None, None, 'tensor'), may hold values from -0.21875 to 0.21875
- out_weight: bfloat16 [2, 768, 768], P(None, 'tensor'), may hold values from -1.25 to 1.25
- up_weight: bfloat16 [2, 768, 3072], P(None, None, 'tensor'), may hold values from -0.21875 to 0.21875
- down_weight: bfloat16 [2, 3072, 768], P(None, 'tensor'), may hold values from -0.109375 to 0.109375
- norm_gain: float32 [2, 2, 768], replicated, may hold values from 0.5 to 1.5
- norm_shift: float32 [2, 2, 768], replicated, may hold values from -3 to 3
- cotangent: bfloat16 [8, 1024, 768], P('dp'), may hold values from -6 to 6
Outputs:
- outputs: bfloat16 [8, 1024, 768], P('dp', 'tensor')
- input_grad: bfloat16 [8, 1024, 768], P('dp', 'tensor')
- qkv_grad: float32 [2, 3, 768, 768], P(None, None, 'dp', 'tensor')
- out_grad: float32 [2, 768, 768], P(None, 'tensor', 'dp')
- up_grad: float32 [2, 768, 3072], P(None, 'dp', 'tensor')
- down_grad: float32 [2, 3072, 768], P(None, 'tensor', 'dp')
- gain_grad: float32 [2, 768], P(None, 'dp')
- shift_grad: float32 [2, 768], P(None, 'dp')
- cross_norm_grad: float32 [2, 2, 768], P(None, None, 'dp')
Inputs may be any that keep to these rules, and one draw needn't show every extreme that they name: `doc_ids`: document ids of a sequence never fall along its segments; a document spans 1 to 4 consecutive segments.
All inputs are finite; a program needn't handle non-finite values.
Results may differ from a plain program's by a relative error of at most 0.022.
Values may be sent and summed in bfloat16 or wider, within the bound.
A program may use at most 128 MiB of HBM per device.

v0:
```python
from functools import partial
import math

import jax
import jax.numpy as jnp
from jax import lax
from jax.sharding import PartitionSpec as P

HEAD_DIM = 64
SEG = 128


EPSILON = 1e-05
MASK_FILL = -1000000000.0


def layer_norm(values, gain_row, shift_row):
    center = jnp.mean(values, axis=-1, keepdims=True)
    offset = values - center
    spread = jnp.mean(offset * offset, axis=-1, keepdims=True)
    inverse = lax.rsqrt(spread + EPSILON)
    scaled = offset * inverse
    return (scaled * gain_row + shift_row, (scaled, inverse))


def norm_back(grad_out, saved, gain_row):
    scaled, inverse = saved
    weighted = grad_out * gain_row
    mean_one = jnp.mean(weighted, axis=-1, keepdims=True)
    mean_two = jnp.mean(weighted * scaled, axis=-1, keepdims=True)
    grad_in = inverse * (weighted - mean_one - scaled * mean_two)
    return (grad_in, jnp.sum(grad_out * scaled, axis=(0, 1)), jnp.sum(grad_out, axis=(0, 1)))


def score_block(head_split, allowed):
    scores = jnp.einsum(
        "bqhe,bkhe->bhqk", head_split[0], head_split[1], preferred_element_type=jnp.float32
    ) * (1.0 / math.sqrt(HEAD_DIM))
    if allowed is not None:
        scores = jnp.where(allowed, scores, MASK_FILL)
    return scores


def attend_forward(rows_low, qkv_local, allowed):
    batch_count = rows_low.shape[0]
    length = rows_low.shape[1]
    project = jnp.einsum(
        "brd,cde->cbre", rows_low, qkv_local, preferred_element_type=jnp.float32
    ).astype(jnp.bfloat16)
    head_split = project.reshape(3, batch_count, length, -1, HEAD_DIM)
    scores = score_block(head_split, allowed)
    log_total = jax.nn.logsumexp(scores, axis=-1)
    soft_low = jnp.exp(scores - log_total[..., None]).astype(jnp.bfloat16)
    mixture = jnp.einsum(
        "bhqk,bkhe->bqhe", soft_low, head_split[2], preferred_element_type=jnp.float32
    )
    return (project, log_total, mixture.astype(jnp.bfloat16).reshape(batch_count, length, -1))


def attend_backward(rows_low, qkv_local, out_local, project, log_total, mixture, grad_low, allowed):
    batch_count = rows_low.shape[0]
    length = rows_low.shape[1]
    head_split = project.reshape(3, batch_count, length, -1, HEAD_DIM)
    grad_mixture = jnp.einsum(
        "brd,fd->brf", grad_low, out_local, preferred_element_type=jnp.float32
    ).astype(jnp.bfloat16)
    out_local_grad = jnp.einsum(
        "brf,brd->fd", mixture, grad_low, preferred_element_type=jnp.float32
    )
    grad_heads = grad_mixture.reshape(batch_count, length, -1, HEAD_DIM)
    scores = score_block(head_split, allowed)
    soft_full = jnp.exp(scores - log_total[..., None])
    grad_soft = jnp.einsum(
        "bqhe,bkhe->bhqk", grad_heads, head_split[2], preferred_element_type=jnp.float32
    )
    row_inner = jnp.sum(grad_soft * soft_full, axis=-1, keepdims=True)
    grad_scores = (soft_full * (grad_soft - row_inner)).astype(jnp.bfloat16)
    scale_factor = 1.0 / math.sqrt(HEAD_DIM)
    grad_query = (
        jnp.einsum(
            "bhqk,bkhe->bqhe", grad_scores, head_split[1], preferred_element_type=jnp.float32
        )
        * scale_factor
    )
    grad_key = (
        jnp.einsum(
            "bhqk,bqhe->bkhe", grad_scores, head_split[0], preferred_element_type=jnp.float32
        )
        * scale_factor
    )
    grad_value = jnp.einsum(
        "bhqk,bqhe->bkhe",
        soft_full.astype(jnp.bfloat16),
        grad_heads,
        preferred_element_type=jnp.float32,
    )
    grad_project = (
        jnp.stack([grad_query, grad_key, grad_value])
        .reshape(3, batch_count, length, -1)
        .astype(jnp.bfloat16)
    )
    qkv_local_grad = jnp.einsum(
        "brd,cbre->cde", rows_low, grad_project, preferred_element_type=jnp.float32
    )
    input_part = jnp.einsum(
        "cbre,cde->brd", grad_project, qkv_local, preferred_element_type=jnp.float32
    )
    return (input_part, qkv_local_grad, out_local_grad)


def expand_forward(rows_low, up_local, down_local):
    upward = jnp.einsum("brd,df->brf", rows_low, up_local, preferred_element_type=jnp.float32)
    active = jax.nn.gelu(upward, approximate=False).astype(jnp.bfloat16)
    return (
        upward,
        active,
        jnp.einsum("brf,fd->brd", active, down_local, preferred_element_type=jnp.float32),
    )


def expand_backward(rows_low, up_local, down_local, upward, active, grad_low):
    grad_active = jnp.einsum(
        "brd,fd->brf", grad_low, down_local, preferred_element_type=jnp.float32
    )
    down_local_grad = jnp.einsum(
        "brf,brd->fd", active, grad_low, preferred_element_type=jnp.float32
    )
    gelu_pull = jax.vjp(partial(jax.nn.gelu, approximate=False), upward)[1]
    grad_upward = gelu_pull(grad_active)[0].astype(jnp.bfloat16)
    up_local_grad = jnp.einsum(
        "brd,brf->df", rows_low, grad_upward, preferred_element_type=jnp.float32
    )
    input_part = jnp.einsum(
        "brf,df->brd", grad_upward, up_local, preferred_element_type=jnp.float32
    )
    return (input_part, up_local_grad, down_local_grad)


def body(
    inputs,
    doc_ids,
    qkv_weight,
    out_weight,
    up_weight,
    down_weight,
    norm_gain,
    norm_shift,
    cotangent,
):
    groups = lax.axis_size("tensor")
    position = lax.axis_index("tensor")
    model_width = inputs.shape[2]
    segment_count = inputs.shape[1] // SEG
    own_count = segment_count // groups
    row_start = position * own_count

    def final_rows(values):
        return lax.dynamic_slice_in_dim(values, row_start, own_count, 0)

    def forward_sum(partial_term):
        return lax.psum(partial_term.astype(jnp.bfloat16), "tensor").astype(jnp.float32)

    def backward_sum(partial_term):
        return lax.psum(partial_term.astype(jnp.bfloat16), "tensor").astype(jnp.float32)

    def cross_sum(partial_term):
        return lax.psum(partial_term.astype(jnp.bfloat16), "tensor").astype(jnp.float32)

    def cross_grad_sum(partial_term):
        return lax.psum(partial_term, "tensor")

    tokens = inputs[0].reshape(segment_count, SEG, model_width)
    tokens_wide = tokens.astype(jnp.float32)
    lower_proj, lower_total, lower_mix = attend_forward(tokens, qkv_weight[0], None)
    attended = forward_sum(
        jnp.einsum("brf,fd->brd", lower_mix, out_weight[0], preferred_element_type=jnp.float32)
    )
    first_norm, first_saved = layer_norm(tokens_wide + attended, norm_gain[0, 0], norm_shift[0, 0])
    first_low = first_norm.astype(jnp.bfloat16)
    lower_up, lower_active, fed_term = expand_forward(first_low, up_weight[0], down_weight[0])
    second, second_saved = layer_norm(
        first_norm + forward_sum(fed_term), norm_gain[0, 1], norm_shift[0, 1]
    )
    summary = second[:, 0, :]
    summary = summary[None]
    same_doc = (doc_ids[0][:, None] == doc_ids[0][None, :])[None, None]
    summary_low = summary.astype(jnp.bfloat16)
    upper_proj, upper_total, upper_mix = attend_forward(summary_low, qkv_weight[1], same_doc)
    upper_att = cross_sum(
        jnp.einsum("brf,fd->brd", upper_mix, out_weight[1], preferred_element_type=jnp.float32)
    )
    upper_first, upper_saved_one = layer_norm(
        summary + upper_att, norm_gain[1, 0], norm_shift[1, 0]
    )
    upper_first_low = upper_first.astype(jnp.bfloat16)
    upper_up, upper_active, upper_fed = expand_forward(
        upper_first_low, up_weight[1], down_weight[1]
    )
    upper_out, upper_saved_two = layer_norm(
        upper_first + cross_sum(upper_fed), norm_gain[1, 1], norm_shift[1, 1]
    )
    joined = second.at[:, 0, :].set(upper_out[0])
    outputs_own = final_rows(joined).reshape(1, -1, model_width).astype(jnp.bfloat16)
    grad_full = cotangent[0].reshape(segment_count, SEG, model_width).astype(jnp.float32)
    grad_top = grad_full[:, 0, :][None]
    grad_upper_fed, gain_cross_two, shift_cross_two = norm_back(
        grad_top, upper_saved_two, norm_gain[1, 1]
    )
    cross_part, up_cross, down_cross = expand_backward(
        upper_first_low,
        up_weight[1],
        down_weight[1],
        upper_up,
        upper_active,
        grad_upper_fed.astype(jnp.bfloat16),
    )
    grad_upper_first = grad_upper_fed + cross_grad_sum(cross_part)
    grad_upper_att, gain_cross_one, shift_cross_one = norm_back(
        grad_upper_first, upper_saved_one, norm_gain[1, 0]
    )
    cross_input_part, qkv_cross, out_cross = attend_backward(
        summary_low,
        qkv_weight[1],
        out_weight[1],
        upper_proj,
        upper_total,
        upper_mix,
        grad_upper_att.astype(jnp.bfloat16),
        same_doc,
    )
    grad_summary = grad_upper_att + cross_grad_sum(cross_input_part)
    grad_second = grad_full.at[:, 0, :].set(grad_summary[0])
    grad_fed, gain_seg_two, shift_seg_two = norm_back(grad_second, second_saved, norm_gain[0, 1])
    fed_low = grad_fed.astype(jnp.bfloat16)
    seg_part, up_seg, down_seg = expand_backward(
        first_low, up_weight[0], down_weight[0], lower_up, lower_active, fed_low
    )
    grad_first = grad_fed + backward_sum(seg_part)
    grad_att, gain_seg_one, shift_seg_one = norm_back(grad_first, first_saved, norm_gain[0, 0])
    att_low = grad_att.astype(jnp.bfloat16)
    seg_input_part, qkv_seg, out_seg = attend_backward(
        tokens, qkv_weight[0], out_weight[0], lower_proj, lower_total, lower_mix, att_low, None
    )
    input_full = grad_att + backward_sum(seg_input_part)
    input_own = final_rows(input_full).reshape(1, -1, model_width).astype(jnp.bfloat16)
    seg_gain = jnp.stack([gain_seg_one, gain_seg_two])
    seg_shift = jnp.stack([shift_seg_one, shift_seg_two])
    cross_norm = jnp.stack(
        [jnp.stack([gain_cross_one, gain_cross_two]), jnp.stack([shift_cross_one, shift_cross_two])]
    )
    qkv_all = jnp.stack([qkv_seg, qkv_cross])
    out_all = jnp.stack([out_seg, out_cross])
    up_all = jnp.stack([up_seg, up_cross])
    down_all = jnp.stack([down_seg, down_cross])
    summed = (
        lax.psum_scatter(qkv_all, "dp", scatter_dimension=2, tiled=True),
        lax.psum_scatter(out_all, "dp", scatter_dimension=2, tiled=True),
        lax.psum_scatter(up_all, "dp", scatter_dimension=1, tiled=True),
        lax.psum_scatter(down_all, "dp", scatter_dimension=2, tiled=True),
        lax.psum_scatter(seg_gain, "dp", scatter_dimension=1, tiled=True),
        lax.psum_scatter(seg_shift, "dp", scatter_dimension=1, tiled=True),
        lax.psum_scatter(cross_norm, "dp", scatter_dimension=2, tiled=True),
    )
    return (
        outputs_own,
        input_own,
        summed[0],
        summed[1],
        summed[2],
        summed[3],
        summed[4],
        summed[5],
        summed[6],
    )


def solution(mesh):
    in_specs = (
        P("dp", None, None),
        P("dp", None),
        P(None, None, None, "tensor"),
        P(None, "tensor", None),
        P(None, None, "tensor"),
        P(None, "tensor", None),
        P(),
        P(),
        P("dp", None, None),
    )
    out_specs = (
        P("dp", "tensor", None),
        P("dp", "tensor", None),
        P(None, None, "dp", "tensor"),
        P(None, "tensor", "dp"),
        P(None, "dp", "tensor"),
        P(None, "tensor", "dp"),
        P(None, "dp"),
        P(None, "dp"),
        P(None, None, "dp"),
    )
    return jax.shard_map(body, mesh=mesh, in_specs=in_specs, out_specs=out_specs, check_vma=False)
```

profile of v0, /device:TPU:0, one launch (start us, length us, event | category | flops | bytes accessed | tf_op | source)
XLA Modules:
  0.0 815.7 jit_solution(13138582783776457540)
XLA Ops:
  7.2 2.8 fusion.10
  12.2 1.8 convolution_convert_fusion.2
  14.8 71.3 %all-reduce.7.cloned.1.call-done = bf16[8,128,768]{2,1,0:T(8,128)(2,1)} async-done(((bf16[8,128,768]{2,1,0:T(8,128)(2,1)}), bf16[8,128,768]{2,1,0:T(8,128)(2,1)}) %all-reduce.7.cloned.1.call-update) | async-done | bytes 1572880 | tf_op jit(solution)/shard_map/psum | solution.py:161
  86.0 2.0 fusion.7
  88.9 2.6 fusion.56
  91.5 7.9 multiply_convert_fusion
  99.4 2.5 convolution_convert_fusion.1
  102.5 1.7 copy-done.7
  105.5 64.8 %all-reduce.9.cloned.1.call-done = bf16[8,128,768]{2,1,0:T(8,128)(2,1)} async-done(((bf16[8,128,768]{2,1,0:T(8,128)(2,1)}), bf16[8,128,768]{2,1,0:T(8,128)(2,1)}) %all-reduce.9.cloned.1.call-update) | async-done | bytes 1572880 | tf_op jit(solution)/shard_map/psum | solution.py:161
  170.3 3.6 fusion.120
  175.2 1.7 copy-done.10
  188.2 18.3 %psum.58 = bf16[1,8,768]{2,0,1:T(2,128)(2,1)} all-reduce(bf16[1,8,768]{2,0,1:T(2,128)(2,1)} %convert_element_type.207), channel_id=1, replica_groups=mesh['dp'=8,'tensor'=4] {'tensor'}, use_global_device_ids=true, to_apply=%region_10.11 | all-reduce | flops 6144 | bytes 24576 | tf_op jit(solution)/shard_map/psum | solution.py:167
  207.9 1.4 fusion.111
  209.9 1.5 fusion.20
  212.0 1.6 fusion.27
  214.2 17.4 %psum.59 = bf16[1,8,768]{2,0,1:T(2,128)(2,1)} all-reduce(bf16[1,8,768]{2,0,1:T(2,128)(2,1)} %convert_element_type.212), channel_id=1, replica_groups=mesh['dp'=8,'tensor'=4] {'tensor'}, use_global_device_ids=true, to_apply=%region_13.14 | all-reduce | flops 6144 | bytes 24576 | tf_op jit(solution)/shard_map/psum | solution.py:167
  232.8 1.8 fusion.72
  234.6 1.6 fusion.117
  236.8 1.7 add_convert_fusion.1
  239.2 1.7 fusion.18
  241.5 18.3 %psum.60 = f32[1,8,768]{2,0,1:T(1,128)} all-reduce(f32[1,8,768]{2,0,1:T(1,128)} %dot_general.130), channel_id=1, replica_groups=mesh['dp'=8,'tensor'=4] {'tensor'}, use_global_device_ids=true, to_apply=%region_18.19 | all-reduce | flops 6144 | bytes 49152 | tf_op jit(solution)/shard_map/psum | solution.py:170
  259.8 1.6 multiply_reduce_fusion.9
  261.4 1.5 fusion.116
  263.4 1.8 convolution_convert_fusion.11
  270.4 1.4 fusion.35
  282.9 1.4 convolution_bitcast_fusion.8
  285.0 17.4 %psum.61 = f32[1,8,768]{2,0,1:T(1,128)} all-reduce(f32[1,8,768]{2,0,1:T(1,128)} %dot_general.138), channel_id=1, replica_groups=mesh['dp'=8,'tensor'=4] {'tensor'}, use_global_device_ids=true, to_apply=%region_22.23 | all-reduce | flops 6144 | bytes 49152 | tf_op jit(solution)/shard_map/psum | solution.py:170
  303.8 1.7 scatter.9
  305.5 3.6 multiply_reduce_fusion
  311.0 2.1 copy-done.19
  313.8 2.2 add_convert_fusion
  317.2 2.6 convolution_convert_fusion
  323.1 2.0 convolution_bitcast_fusion
  325.1 5.4 convolution_bitcast_fusion.2
  330.6 57.5 %all-reduce.11.cloned.1.call-done = bf16[8,128,768]{2,1,0:T(8,128)(2,1)} async-done(((bf16[8,128,768]{2,1,0:T(8,128)(2,1)}), bf16[8,128,768]{2,1,0:T(8,128)(2,1)}) %all-reduce.11.cloned.1.call-update) | async-done | bytes 1572880 | tf_op jit(solution)/shard_map/psum | solution.py:164
  388.1 4.1 multiply_reduce_fusion.1
  392.8 1.6 copy.107
  397.0 1.6 copy.109
  398.7 4.9 pad_maximum_fusion.1
  403.6 8.2 %copy.89 = f32[2,768,768]{1,0,2:T(2,128)} copy(f32[2,768,768]{2,1,0:T(8,128)} %pad_maximum_fusion.1) | data formatting | bytes 9437184 | tf_op jit(solution)/shard_map/stack | solution.py:254
  413.3 3.1 subtract_multiply_fusion
  417.1 1.8 copy-done.1
  422.4 2.7 bitcast_convert_fusion
  426.2 2.4 convolution_bitcast_fusion.7
  429.7 3.5 copy.105
  433.2 3.3 reshape.677
  438.0 2.2 convolution_bitcast_fusion.5
  440.2 2.0 pad_maximum_fusion.2
  442.2 6.9 copy.103
  449.1 8.0 reshape.675
  458.4 3.3 convolution_bitcast_fusion.3
  461.7 2.4 pad_maximum_fusion
  466.0 1.7 scatter.6
  467.7 1.9 dynamic-slice_convert_fusion
  471.2 1.4 copy.108
  472.6 25.5 %reduce-scatter.25.cloned.1.call-done = f32[96,2]{1,0:T(8,128)} async-done(((f32[768,2]{1,0:T(8,128)}), f32[96,2]{1,0:T(8,128)}) %reduce-scatter.25.cloned.1.call-update) | async-done | bytes 784
  498.1 1.4 copy.110
  499.5 88.7 %all-reduce.15.cloned.1.call-done = f32[2,768,768]{1,0,2:T(2,128)} async-done(((f32[2,768,768]{1,0,2:T(2,128)}), f32[2,768,768]{1,0,2:T(2,128)}) %all-reduce.15.cloned.1.call-update) | async-done | bytes 4718608
  590.2 69.7 %all-reduce.13.cloned.1.call-done = bf16[8,128,768]{2,1,0:T(8,128)(2,1)} async-done(((bf16[8,128,768]{2,1,0:T(8,128)(2,1)}), bf16[8,128,768]{2,1,0:T(8,128)(2,1)}) %all-reduce.13.cloned.1.call-update) | async-done | bytes 1572880 | tf_op jit(solution)/shard_map/psum | solution.py:164
  660.0 2.0 fusion.50
  662.0 37.4 %reduce-scatter.21.cloned.1.call-done = f32[96,384]{1,0:T(8,128)} async-done(((f32[768,384]{1,0:T(8,128)}), f32[96,384]{1,0:T(8,128)}) %reduce-scatter.21.cloned.1.call-update) | async-done | bytes 147472
  701.3 49.5 %reduce-scatter.19.cloned.1.call-done = f32[96,1152]{1,0:T(8,128)} async-done(((f32[768,1152]{1,0:T(8,128)}), f32[96,1152]{1,0:T(8,128)}) %reduce-scatter.19.cloned.1.call-update) | async-done | bytes 442384
  750.8 1.6 reshape.676
  753.4 55.4 %reduce-scatter.17.cloned.1.call-done = f32[2,96,768]{2,1,0:T(8,128)} async-done(((f32[2,768,768]{2,1,0:T(8,128)}), f32[2,96,768]{2,1,0:T(8,128)}) %reduce-scatter.17.cloned.1.call-update) | async-done | bytes 589840 | tf_op jit(solution)/shard_map/reduce_scatter | solution.py:258
  (274 shorter events, 71.4 us)
Async XLA Ops:
  7.2 78.9 %all-reduce.7.cloned.1.call-start = ((), (), s32[]{:S(2)}) async-start(), calls=%async_computation.6 | async-start | bytes 3145728 | tf_op jit(solution)/shard_map/psum | solution.py:161
  10.1 2.0 copy-start.11
  10.1 2.0 copy-start.13
  10.1 2.0 copy-start.22
  10.9 3.2 copy-start.68
  10.9 3.2 copy-start.69
  11.0 75.1 %copy-start.2 = (bf16[1,1024,768]{2,1,0:T(8,128)(2,1)S(1)}, bf16[1,1024,768]{2,1,0:T(8,128)(2,1)}, u32[]{:S(2)}) copy-start(bf16[1,1024,768]{2,1,0:T(8,128)(2,1)} %param.13) | copy-start | bytes 4718596
  12.2 75.9 %copy-start.15 = (bf16[8,3,64,128]{3,2,1,0:T(8,128)(2,1)}, bf16[8,3,64,128]{3,2,1,0:T(8,128)(2,1)S(1)}, u32[]{:S(2)}) copy-start(bf16[8,3,64,128]{3,2,1,0:T(8,128)(2,1)S(1)} %convolution_convert_fusion.6) | copy-start | bytes 1179652
  14.1 156.3 %all-reduce.9.cloned.1.call-start = ((), (), s32[]{:S(2)}) async-start(), calls=%async_computation.7 | async-start | bytes 3145728 | tf_op jit(solution)/shard_map/psum | solution.py:161
  14.8 74.1 %copy-start.45 = (f32[768]{0:T(1024)}, f32[768]{0:T(1024)S(1)}, u32[]{:S(2)}) copy-start(f32[768]{0:T(1024)S(1)} %get-tuple-element.118) | copy-start | bytes 9220
  14.8 74.1 %copy-start.59 = (f32[768]{0:T(1024)}, f32[768]{0:T(1024)S(1)}, u32[]{:S(2)}) copy-start(f32[768]{0:T(1024)S(1)} %get-tuple-element.83) | copy-start | bytes 9220
  86.0 2.1 copy-start.4
  86.0 2.9 copy-start.20
  88.1 3.4 copy-start.33
  88.9 2.6 copy-start.47
  91.5 7.9 copy-start.17
  91.5 7.9 copy-start.73
  99.4 2.5 copy-start.27
  99.4 2.8 copy-start.26
  102.0 2.9 copy-start.71
  102.0 286.1 %all-reduce.11.cloned.1.call-start = ((), (), s32[]{:S(2)}) async-start(), calls=%async_computation.8 | async-start | bytes 3145728 | tf_op jit(solution)/shard_map/psum | solution.py:164
  102.5 1.7 copy-start.7
  174.6 2.3 copy-start.24
  175.1 1.7 copy-start.10
  207.9 1.4 copy-start.72
  305.5 3.6 copy-start.8
  305.5 3.6 copy-start.36
  305.5 3.6 copy-start.50
  305.5 3.6 copy-start.52
  309.1 1.9 copy-start.18
  309.1 4.0 copy-start.19
  309.1 4.7 copy-start.74
  310.1 5.9 copy-start.9
  313.8 3.3 copy-start.21
  317.1 2.9 copy-start.64
  317.1 2.9 copy-start.67
  317.1 3.5 copy-start.66
  317.1 4.1 copy-start.63
  317.1 4.1 copy-start.65
  317.1 4.1 copy-start.62
  319.7 3.3 copy-start.41
  319.7 3.3 copy-start.54
  319.8 149.8 %reduce-scatter.27.cloned.1.call-start = ((), (), s32[]{:S(2)}) async-start(), calls=%async_computation.15 | async-start | bytes 442368
  325.1 63.0 %copy-start.3 = (bf16[1,1024,768]{2,1,0:T(8,128)(2,1)S(1)}, bf16[1,1024,768]{2,1,0:T(8,128)(2,1)}, u32[]{:S(2)}) copy-start(bf16[1,1024,768]{2,1,0:T(8,128)(2,1)} %param.13) | copy-start | bytes 4718596
  325.1 63.0 %copy-start.5 = (bf16[8,128,768]{2,1,0:T(8,128)(2,1)S(1)}, bf16[8,128,768]{2,1,0:T(8,128)(2,1)}, u32[]{:S(2)}) copy-start(bf16[8,128,768]{2,1,0:T(8,128)(2,1)} %all-reduce.7.cloned.1.call-done) | copy-start | bytes 4718596
  330.5 140.7 %reduce-scatter.23.cloned.1.call-start = ((), (), s32[]{:S(2)}) async-start(), calls=%async_computation.13 | async-start | bytes 442368
  388.1 4.1 copy-start.70
  395.7 102.4 %reduce-scatter.25.cloned.1.call-start = ((), (), s32[]{:S(2)}) async-start(), calls=%async_computation.14 | async-start | bytes 442368
  398.7 189.6 %all-reduce.15.cloned.1.call-start = ((), (), s32[]{:S(2)}) async-start(), calls=%async_computation.16 | async-start | bytes 9437184
  411.8 248.1 %all-reduce.13.cloned.1.call-start = ((), (), s32[]{:S(2)}) async-start(), calls=%async_computation.9 | async-start | bytes 3145728 | tf_op jit(solution)/shard_map/psum | solution.py:164
  413.3 3.1 copy-start.23
  416.4 3.1 copy-start.6
  416.4 2.5 copy-start.1
  416.4 2.6 copy-start.14
  420.0 2.4 copy-start.25
  422.4 2.8 copy-start.57
  422.4 3.8 copy-start.16
  425.1 274.3 %reduce-scatter.21.cloned.1.call-start = ((), (), s32[]{:S(2)}) async-start(), calls=%async_computation.12 | async-start | bytes 1327104
  429.7 7.1 copy-start.44
  433.2 4.8 copy-start.29
  436.5 314.3 %reduce-scatter.19.cloned.1.call-start = ((), (), s32[]{:S(2)}) async-start(), calls=%async_computation.11 | async-start | bytes 3981312
  457.1 1.3 copy-start.48
  457.1 351.6 %reduce-scatter.17.cloned.1.call-start = ((), (), s32[]{:S(2)}) async-start(), calls=%async_computation.10 | async-start | bytes 5308416 | tf_op jit(solution)/shard_map/reduce_scatter | solution.py:258
  464.1 1.9 copy-start.42
  (24 other events, 20.2 us)
Sparse Core Ops, SparseCore 0:
  14.2 71.8 all-reduce.6
  102.1 68.1 all-reduce.8
  319.9 68.1 all-reduce.10
  391.0 32.8 reduce-scatter.26
  427.4 33.8 reduce-scatter.22
  464.2 33.8 reduce-scatter.24
  501.4 86.7 all-reduce.14
  590.8 69.1 all-reduce.12
  663.5 35.8 reduce-scatter.20
  702.7 48.0 reduce-scatter.18
  754.9 53.8 reduce-scatter.16
where the time goes:
time: 826 us; the launch traced here: 816 us
  waiting for transfers between devices  520 us (63%)
  local copies, waits for them, and re-layouts  93.7 us (11%)
  blocking collectives  71.4 us (9%)
  other arithmetic  57.4 us (7%)
  matrix products  56.3 us (7%)
  between operations  16 us (2%)
    unnamed x17, waiting for transfers between devices  201 us
    psum x2, waiting for transfers between devices, forward_sum(): lax.psum(partial_term.astype(jnp.bfloat16), 'tensor').astype(jnp.float32)  136 us
    psum x2, waiting for transfers between devices, backward_sum(): lax.psum(partial_term.astype(jnp.bfloat16), 'tensor').astype(jnp.float32)  127 us
    unnamed x175, local copies, waits for them, and re-layouts  57.8 us
    reduce_scatter x1, waiting for transfers between devices, body(): lax.psum_scatter(up_all, 'dp', scatter_dimension=1, tiled=True)  55.4 us
    psum x2, blocking collectives, cross_sum(): lax.psum(partial_term.astype(jnp.bfloat16), 'tensor').astype(jnp.float32)  35.7 us
    psum x2, blocking collectives, cross_grad_sum(): return lax.psum(partial_term, 'tensor')  35.7 us
  transfers between devices with their start and end apart: 11, of which 9 were waited for; matrix products, arithmetic and copies ran while one was open for 12% of the time, Pallas kernels for 0%

commit v1 on v0

--- a/solution.py
+++ b/solution.py
@@ -4,6 +4,8 @@
 import jax
 import jax.numpy as jnp
 from jax import lax
+from jax.experimental import pallas as pl
+from jax.experimental.pallas import tpu as pltpu
 from jax.sharding import PartitionSpec as P
 
 HEAD_DIM = 64
@@ -274,6 +276,830 @@
     )
 
 
+MESH = pl.DeviceIdType.MESH
+F32 = jnp.float32
+BF16 = jnp.bfloat16
+SCALE = 1.0 / math.sqrt(HEAD_DIM)
+ATT, UP, DOWN = 0, 1, 2
+BLK = 96
+HALF = 48
+
+
+def mm(a, b):
+    return lax.dot_general(a, b, (((1,), (0,)), ((), ())), preferred_element_type=F32)
+
+
+def mm_nt(a, b):
+    return lax.dot_general(a, b, (((1,), (1,)), ((), ())), preferred_element_type=F32)
+
+
+def mm_tn(a, b):
+    return lax.dot_general(a, b, (((0,), (0,)), ((), ())), preferred_element_type=F32)
+
+
+def normalize(values):
+    center = jnp.mean(values, axis=-1, keepdims=True)
+    offset = values - center
+    spread = jnp.mean(offset * offset, axis=-1, keepdims=True)
+    inverse = lax.rsqrt(spread + EPSILON)
+    return offset * inverse, inverse
+
+
+def normalize_back(grad_out, scaled, inverse, gain_row):
+    weighted = grad_out * gain_row
+    mean_one = jnp.mean(weighted, axis=-1, keepdims=True)
+    mean_two = jnp.mean(weighted * scaled, axis=-1, keepdims=True)
+    return inverse * (weighted - mean_one - scaled * mean_two)
+
+
+def gelu_pair(upward):
+    cdf = 0.5 * (1.0 + lax.erf(upward * math.sqrt(0.5)))
+    pdf = jnp.exp(upward * upward * -0.5) * (1.0 / math.sqrt(2.0 * math.pi))
+    return upward * cdf, cdf + upward * pdf
+
+
+def fused_kernel(
+    tokens_hbm, cot_hbm, cot_seg, allowed_ref, wa_hbm, wu_hbm, wd_hbm, gain_ref, shift_ref,
+    out_ref, ing_ref, qkvg_ref, outg_ref, upg_ref, downg_ref, gaing_ref, shiftg_ref, crossg_ref,
+    W, G, RC, RA1, RB1, RA2, RB2, RZ, L1, X, COT, QKV, PR, MIX, ACT, DG, GU, GQ, ACC, SC1, SC2, GF,
+    FL, FLT, FDL, FDLT, XT, GM, C8, INV1, INV2, FAC, LT, EL, ER, E, NV, SV, RSV,
+    sem_local, ag_s, ag_r, rs_s, rs_r, e_s, e_r, f_s, f_r, v_s, v_r,
+):
+    dp = lax.axis_index("dp")
+    z = lax.axis_index("tensor")
+    c = dp % 2
+    x = (dp // 2) % 2
+    y = dp // 4
+    nc, nx, ny = 1 - c, 1 - x, 1 - y
+    core_peer = (dp + 1 - 2 * c, z)
+    x_peer = (dp + 2 - 4 * x, z)
+    y_peer = (dp + 4 - 8 * y, z)
+    z_peer = [None, (dp, z + 1 - 2 * (z % 2)), (dp, z + 2 - 4 * (z // 2)), (dp, 3 - z)]
+    z_of = [z, z + 1 - 2 * (z % 2), z + 2 - 4 * (z // 2), 3 - z]
+
+    def plane_index(m):
+        ty = y if m // 4 == 0 else ny
+        tx = x if (m // 2) % 2 == 0 else nx
+        tc = c if m % 2 == 0 else nc
+        return ty * 4 + tx * 2 + tc
+
+    sends = []
+    waited = []
+
+    def remote(src, dst, ssem, rsem, target):
+        copy = pltpu.make_async_remote_copy(
+            src_ref=src, dst_ref=dst, send_sem=ssem, recv_sem=rsem, device_id=target, device_id_type=MESH
+        )
+        copy.start()
+        sends.append(copy)
+        return copy
+
+    loads = {}
+
+    def load(name, index, src, dst):
+        copy = pltpu.make_async_copy(src, dst, sem_local.at[index])
+        copy.start()
+        loads[name] = copy
+
+    load("x", 0, tokens_hbm.at[0, pl.ds(pl.multiple_of(z * 256, 256), 256)], X)
+    load("wa", 1, wa_hbm.at[0], W.at[ATT, 0])
+    load("wu", 2, wu_hbm.at[0], W.at[UP, 0])
+    load("wd", 3, wd_hbm.at[0], W.at[DOWN, 0])
+    load("cot", 4, cot_hbm.at[0, pl.ds(pl.multiple_of(z * 256, 256), 256)], COT)
+    load("l1a", 5, wa_hbm.at[1], L1.at[ATT])
+    load("l1u", 6, wu_hbm.at[1], L1.at[UP])
+    load("l1d", 7, wd_hbm.at[1], L1.at[DOWN])
+    load("c8", 8, cot_seg.at[:, pl.ds(0, 16)], C8)
+
+    barrier = pltpu.get_barrier_semaphore()
+    for m in range(1, 8):
+        pl.semaphore_signal(barrier, inc=1, device_id=(plane_index(m), z), device_id_type=MESH)
+    for r in range(1, 4):
+        pl.semaphore_signal(barrier, inc=1, device_id=z_peer[r], device_id_type=MESH)
+    pl.semaphore_wait(barrier, 10)
+
+    own_hbm = [wa_hbm.at[0], wu_hbm.at[0], wd_hbm.at[0]]
+    units = [(ATT, 1), (ATT, 2), (ATT, 3), (UP, 1), (DOWN, 1), (UP, 2), (DOWN, 2), (UP, 3), (DOWN, 3)]
+    zc, a1, b1, a2, b2, cc = {}, {}, {}, {}, {}, {}
+    for i, (k, r) in enumerate(units):
+        zc[i] = remote(
+            own_hbm[k].at[y, x, c], W.at[k, r, y, x, c], ag_s.at[0, i], ag_r.at[0, i], z_peer[r]
+        )
+
+    def gather_tick(t):
+        i = t
+        if 0 <= i < 9:
+            k, r = units[i]
+            zc[i].wait_recv()
+            part = W.at[k, r, y, x, c, pl.ds(0, HALF)]
+            a1[i] = remote(part, part, ag_s.at[1, i], ag_r.at[1, i], x_peer)
+            part = W.at[k, r, y, x, c, pl.ds(HALF, HALF)]
+            b1[i] = remote(part, part, ag_s.at[2, i], ag_r.at[2, i], y_peer)
+        i = t - 1
+        if 0 <= i < 9:
+            k, r = units[i]
+            a1[i].wait_recv()
+            part = W.at[k, r, y, :, c, pl.ds(0, HALF)]
+            a2[i] = remote(part, part, ag_s.at[3, i], ag_r.at[3, i], y_peer)
+            b1[i].wait_recv()
+            part = W.at[k, r, :, x, c, pl.ds(HALF, HALF)]
+            b2[i] = remote(part, part, ag_s.at[4, i], ag_r.at[4, i], x_peer)
+        i = t - 2
+        if 0 <= i < 9:
+            k, r = units[i]
+            a2[i].wait_recv()
+            b2[i].wait_recv()
+            part = W.at[k, r, :, :, c]
+            cc[i] = remote(part, part, ag_s.at[5, i], ag_r.at[5, i], core_peer)
+        i = t - 3
+        if 0 <= i < 9:
+            cc[i].wait_recv()
+
+    def unit_value(ref):
+        return ref[...].reshape(768, ref.shape[-1])
+
+    def cols(k, r, start, size):
+        return unit_value(W.at[k, r, :, :, :, :, pl.ds(start, size)])
+
+    def accumulate(first, value):
+        if first:
+            ACC[...] = value
+        else:
+            ACC[...] += value
+
+    def attn_forward(r):
+        QKV[r] = mm(X[...], cols(ATT, r, 0, 576)).astype(BF16)
+
+        def segment(s, carry):
+            rows = pl.ds(pl.multiple_of(s * SEG, SEG), SEG)
+            qkv = QKV[r, rows, :]
+            mixes = []
+            for h in range(3):
+                q = qkv[:, h * 64 : h * 64 + 64]
+                key = qkv[:, 192 + h * 64 : 256 + h * 64]
+                val = qkv[:, 384 + h * 64 : 448 + h * 64]
+                scores = mm_nt(q, key) * SCALE
+                top = jnp.max(scores, axis=-1, keepdims=True)
+                expd = jnp.exp(scores - top)
+                prob = expd * (1.0 / jnp.sum(expd, axis=-1, keepdims=True))
+                PR[r, h, rows, :] = prob
+                mixes.append(mm(prob.astype(BF16), val))
+            MIX[r, rows, :] = jnp.concatenate(mixes, axis=-1).astype(BF16)
+            return carry
+
+        lax.fori_loop(0, 2, segment, 0)
+        accumulate(r == 0, mm_nt(MIX[r], cols(ATT, r, 576, 192)))
+
+    def row_chunks(body, init=0):
+        def one(i, carry):
+            return body(i, pl.ds(pl.multiple_of(i * 64, 64), 64), carry)
+
+        return lax.fori_loop(0, 4, one, init)
+
+    g00, g01 = gain_ref[0, 0:1, :], gain_ref[0, 1:2, :]
+    b00, b01 = shift_ref[0, 0:1, :], shift_ref[0, 1:2, :]
+    g10, g11 = gain_ref[1, 0:1, :], gain_ref[1, 1:2, :]
+    b10, b11 = shift_ref[1, 0:1, :], shift_ref[1, 1:2, :]
+
+    def norm_one():
+        def chunk(i, rows, carry):
+            scaled, inverse = normalize(X[rows, :].astype(F32) + ACC[rows, :])
+            SC1[rows, :] = scaled
+            INV1[rows, :] = jnp.broadcast_to(inverse, (64, 128))
+            FL[rows, :] = (scaled * g00 + b00).astype(BF16)
+            return carry
+
+        row_chunks(chunk)
+
+    def ffn_forward(r):
+        def block(n, carry):
+            part = pl.ds(pl.multiple_of(n * 256, 256), 256)
+            upward = mm(FL[...], unit_value(W.at[UP, r, :, :, :, :, part]))
+            active, slope = gelu_pair(upward)
+            ACT[r, :, part] = active.astype(BF16)
+            DG[r, :, part] = slope.astype(DG.dtype)
+            return carry
+
+        lax.fori_loop(0, 3, block, 0)
+
+    def ffn_down(r):
+        accumulate(r == 0, mm(ACT[r], cols(DOWN, r, 0, 768)))
+
+    def norm_two():
+        def chunk(i, rows, carry):
+            first = SC1[rows, :] * g00 + b00
+            scaled, inverse = normalize(first + ACC[rows, :])
+            SC2[rows, :] = scaled
+            INV2[rows, :] = jnp.broadcast_to(inverse, (64, 128))
+            out_ref[0, rows, :] = (scaled * g01 + b01).astype(BF16)
+            return carry
+
+        row_chunks(chunk)
+
+    def transpose_into(dst, src):
+        for i in range(2):
+            dst[:, i * 128 : i * 128 + 128] = src[i * 128 : i * 128 + 128, :].T
+
+    loads["x"].wait()
+    loads["wa"].wait()
+    attn_forward(0)
+    gather_tick(0)
+    gather_tick(1)
+    transpose_into(XT, X)
+    gather_tick(2)
+    gather_tick(3)
+    attn_forward(1)
+    gather_tick(4)
+    attn_forward(2)
+    gather_tick(5)
+    attn_forward(3)
+    norm_one()
+    loads["wu"].wait()
+    loads["wd"].wait()
+    gather_tick(6)
+    ffn_forward(0)
+    ffn_down(0)
+    gather_tick(7)
+    ffn_forward(1)
+    ffn_down(1)
+    gather_tick(8)
+    transpose_into(FLT, FL)
+    gather_tick(9)
+    ffn_forward(2)
+    ffn_down(2)
+    gather_tick(10)
+    ffn_forward(3)
+    gather_tick(11)
+    ffn_down(3)
+    norm_two()
+
+    exch = {}
+
+    def exchange(e, value):
+        E[e, 0] = value
+        for r in range(1, 4):
+            exch[e, r] = remote(E.at[e, 0], E.at[e, r], e_s.at[e, r - 1], e_r.at[e, r - 1], z_peer[r])
+
+    def exchange_wait(e):
+        for r in range(1, 4):
+            exch[e, r].wait_recv()
+
+    def exchange_sum(e):
+        exchange_wait(e)
+        return (E[e, 0] + E[e, 1]) + (E[e, 2] + E[e, 3])
+
+    row_of = lax.broadcasted_iota(jnp.int32, (8, 768), 0)
+    pair_of = row_of // 2
+
+    def assemble(e, start):
+        total = None
+        for r in range(4):
+            two = E[e, r][start : start + 2, :]
+            four = jnp.concatenate([two, two, two, two], axis=0)
+            part = jnp.where(pair_of == z_of[r], four, 0.0)
+            total = part if total is None else total + part
+        return total
+
+    def own_row(value, j):
+        return jnp.sum(jnp.where(row_of == 2 * z + j, value, 0.0), axis=0, keepdims=True)
+
+    def two_rows(ref):
+        return jnp.concatenate([ref[0:1, :], ref[128:129, :]], axis=0)
+
+    inv_two = jnp.broadcast_to(two_rows(INV2)[:, 0:1], (2, 768))
+    first_two = two_rows(SC1) * g00 + b00
+    exchange(0, jnp.concatenate([two_rows(SC2), first_two, inv_two, inv_two], axis=0))
+
+    loads["cot"].wait()
+
+    def norm_two_back():
+        def chunk(i, rows, carry):
+            gains, shifts = carry
+            which = lax.broadcasted_iota(jnp.int32, (64, 768), 0) + i * 64
+            grad = jnp.where(which % SEG == 0, 0.0, COT[rows, :].astype(F32))
+            scaled = SC2[rows, :]
+            fed = normalize_back(grad, scaled, INV2[rows, 0:1], g01)
+            GF[rows, :] = fed
+            FDL[rows, :] = fed.astype(BF16)
+            return (
+                gains + jnp.sum(grad * scaled, axis=0, keepdims=True),
+                shifts + jnp.sum(grad, axis=0, keepdims=True),
+            )
+
+        zero = jnp.zeros((1, 768), F32)
+        gains, shifts = row_chunks(chunk, (zero, zero))
+        NV[1:2, :] = gains
+        NV[3:4, :] = shifts
+
+    norm_two_back()
+    transpose_into(FDLT, FDL)
+
+    def grad_unit(k, r):
+        return W.at[UP, r] if k == ATT else G.at[k - 1, r]
+
+    order = [(DOWN, 1), (UP, 1), (DOWN, 2), (UP, 2), (DOWN, 3), (UP, 3), (DOWN, 0), (UP, 0)]
+    order += [(ATT, 1), (ATT, 2), (ATT, 3), (ATT, 0)]
+    s0, sa1, sb1, sa2, sb2, sz = {}, {}, {}, {}, {}, {}
+
+    def sum_start(i):
+        k, r = order[i]
+        g = grad_unit(k, r)
+        s0[i] = remote(g.at[:, :, nc], RC.at[i], rs_s.at[0, i], rs_r.at[0, i], core_peer)
+
+    def add_low(a, b):
+        return (a.astype(F32) + b.astype(F32)).astype(BF16)
+
+    def sum_one(i):
+        if not 0 <= i < 12:
+            return
+        k, r = order[i]
+        g = grad_unit(k, r)
+        s0[i].wait_recv()
+
+        def block(j, carry):
+            jy, jx = j // 2, j % 2
+            g[jy, jx, c] = add_low(g[jy, jx, c], RC[i, jy, jx])
+            return carry
+
+        lax.fori_loop(0, 4, block, 0)
+        sa1[i] = remote(g.at[:, nx, c, pl.ds(0, HALF)], RA1.at[i], rs_s.at[1, i], rs_r.at[1, i], x_peer)
+        sb1[i] = remote(g.at[ny, :, c, pl.ds(HALF, HALF)], RB1.at[i], rs_s.at[2, i], rs_r.at[2, i], y_peer)
+
+    def sum_two(i):
+        if not 0 <= i < 12:
+            return
+        k, r = order[i]
+        g = grad_unit(k, r)
+        sa1[i].wait_recv()
+        for j in range(2):
+            g[j, x, c, 0:HALF, :] = add_low(g[j, x, c, 0:HALF, :], RA1[i, j])
+        sa2[i] = remote(g.at[ny, x, c, pl.ds(0, HALF)], RA2.at[i], rs_s.at[3, i], rs_r.at[3, i], y_peer)
+        sb1[i].wait_recv()
+        for j in range(2):
+            g[y, j, c, HALF:BLK, :] = add_low(g[y, j, c, HALF:BLK, :], RB1[i, j])
+        sb2[i] = remote(g.at[y, nx, c, pl.ds(HALF, HALF)], RB2.at[i], rs_s.at[4, i], rs_r.at[4, i], x_peer)
+
+    def sum_three(i):
+        if not 0 <= i < 12:
+            return
+        k, r = order[i]
+        g = grad_unit(k, r)
+        sa2[i].wait_recv()
+        g[y, x, c, 0:HALF, :] = add_low(g[y, x, c, 0:HALF, :], RA2[i])
+        sb2[i].wait_recv()
+        g[y, x, c, HALF:BLK, :] = add_low(g[y, x, c, HALF:BLK, :], RB2[i])
+        if r:
+            sz[k, r] = remote(g.at[y, x, c], RZ.at[k, r - 1], rs_s.at[5, i], rs_r.at[5, i], z_peer[r])
+
+    def pump(i):
+        sum_one(i)
+        sum_two(i - 1)
+        sum_three(i - 2)
+
+    def sum_final(k):
+        for r in range(1, 4):
+            sz[k, r].wait_recv()
+        g = grad_unit(k, 0)
+        own = g[y, x, c].astype(F32) + RZ[k, 0].astype(F32)
+        return own + (RZ[k, 1].astype(F32) + RZ[k, 2].astype(F32))
+
+    def store_unit(ref, parts):
+        for start, size, value in parts:
+            ref[:, :, :, :, start : start + size] = value().astype(BF16).reshape(2, 2, 2, BLK, size)
+
+    def store_ffn(k, r, lhs_t, rhs, extra=None):
+        ref = grad_unit(k, r)
+
+        def block(n, carry):
+            part = pl.ds(pl.multiple_of(n * 256, 256), 256)
+            value = mm(lhs_t[...], rhs[:, part])
+            if extra is not None:
+                value = value + mm(extra[0][...], extra[1][:, part])
+            ref[:, :, :, :, part] = value.astype(BF16).reshape(2, 2, 2, BLK, 256)
+            return carry
+
+        lax.fori_loop(0, 3, block, 0)
+
+    def ffn_back_one(r):
+        ga = mm_nt(FDL[...], cols(DOWN, r, 0, 768))
+        GU[...] = (ga * DG[r].astype(F32)).astype(BF16)
+
+    def ffn_back_two(r, first):
+        accumulate(first, mm_nt(GU[...], cols(UP, r, 0, 768)))
+
+    def l1(k, start, size):
+        return unit_value(L1.at[k, :, :, :, :, pl.ds(start, size)])
+
+    live = {}
+
+    def cross_one():
+        exchange_wait(0)
+        live["sc2"] = assemble(0, 0)
+        first8 = assemble(0, 2)
+        live["inv2"] = assemble(0, 4)[:, 0:1]
+        summary = live["sc2"] * g01 + b01
+        live["summary"] = summary
+        live["summary_low"] = summary.astype(BF16)
+        live["first8_low"] = first8.astype(BF16)
+        loads["l1a"].wait()
+        qkv = mm(live["summary_low"], l1(ATT, 0, 576)).astype(BF16).astype(F32)
+        pad = jnp.zeros((120, 64), F32)
+        keep = allowed_ref[...] > 0.5
+        mixes = []
+        for h in range(3):
+            q = qkv[:, h * 64 : h * 64 + 64].astype(BF16)
+            key = jnp.concatenate([qkv[:, 192 + h * 64 : 256 + h * 64], pad], axis=0).astype(BF16)
+            val = jnp.concatenate([qkv[:, 384 + h * 64 : 448 + h * 64], pad], axis=0).astype(BF16)
+            scores = jnp.where(keep, mm_nt(q, key) * SCALE, MASK_FILL)
+            top = jnp.max(scores, axis=-1, keepdims=True)
+            expd = jnp.exp(scores - top)
+            prob = expd * (1.0 / jnp.sum(expd, axis=-1, keepdims=True))
+            live["prob", h], live["q", h], live["key", h], live["val", h] = prob, q, key, val
+            mixes.append(mm(prob.astype(BF16), val))
+        mix = jnp.concatenate(mixes, axis=-1).astype(BF16)
+        live["mix"] = mix
+        exchange(1, mm_nt(mix, l1(ATT, 576, 192)))
+
+    def cross_two():
+        attended = exchange_sum(1)
+        live["xs1"], live["xi1"] = normalize(live["summary"] + attended)
+        first = live["xs1"] * g10 + b10
+        live["xfirst"] = first
+        live["xfirst_low"] = first.astype(BF16)
+        loads["l1u"].wait()
+        loads["l1d"].wait()
+        active, live["xdg"] = gelu_pair(mm(live["xfirst_low"], l1(UP, 0, 768)))
+        live["xact"] = active.astype(BF16)
+        exchange(2, mm(live["xact"], l1(DOWN, 0, 768)))
+
+    def cross_three():
+        fed = exchange_sum(2)
+        xs2, xi2 = normalize(live["xfirst"] + fed)
+        upper = xs2 * g11 + b11
+        for j in range(2):
+            out_ref[0, j * 128 : j * 128 + 1, :] = own_row(upper, j).astype(BF16)
+        loads["c8"].wait()
+        grad_top = C8[...].astype(F32)[:, 0, :]
+        live["xs2"], live["xi2"] = xs2, xi2
+        grad_fed = normalize_back(grad_top, live["xs2"], live["xi2"], g11)
+        NV[5:6, :] = jnp.sum(grad_top * live["xs2"], axis=0, keepdims=True)
+        NV[7:8, :] = jnp.sum(grad_top, axis=0, keepdims=True)
+        live["xgf"] = grad_fed
+        live["xfed_low"] = grad_fed.astype(BF16)
+        ga = mm_nt(live["xfed_low"], l1(DOWN, 0, 768))
+        live["xgu"] = (ga * live["xdg"]).astype(BF16)
+        exchange(3, mm_nt(live["xgu"], l1(UP, 0, 768)))
+
+    def cross_four():
+        grad_first = live["xgf"] + exchange_sum(3)
+        grad_att = normalize_back(grad_first, live["xs1"], live["xi1"], g10)
+        NV[4:5, :] = jnp.sum(grad_first * live["xs1"], axis=0, keepdims=True)
+        NV[6:7, :] = jnp.sum(grad_first, axis=0, keepdims=True)
+        live["xga"] = grad_att
+        att_low = grad_att.astype(BF16)
+        live["xatt_low"] = att_low
+        gm = mm(att_low, l1(ATT, 576, 192)).astype(BF16)
+        gqs, gks, gvs = [], [], []
+        for h in range(3):
+            gmh = gm[:, h * 64 : h * 64 + 64]
+            prob = live["prob", h]
+            gp = mm_nt(gmh, live["val", h])
+            inner = jnp.sum(gp * prob, axis=-1, keepdims=True)
+            gs = (prob * (gp - inner)).astype(BF16)
+            gqs.append(mm(gs, live["key", h]) * SCALE)
+            gks.append(mm_tn(gs, live["q", h])[0:8, :] * SCALE)
+            gvs.append(mm_tn(prob.astype(BF16), gmh)[0:8, :])
+        gqkv = jnp.concatenate(gqs + gks + gvs, axis=-1).astype(BF16)
+        live["xgqkv"] = gqkv
+        exchange(4, mm_nt(gqkv, l1(ATT, 0, 576)))
+
+    def cross_five():
+        grad_summary = live["xga"] + exchange_sum(4)
+        mine = jnp.where(pair_of == z, grad_summary, 0.0)
+        NV[1:2, :] += jnp.sum(mine * live["sc2"], axis=0, keepdims=True)
+        NV[3:4, :] += jnp.sum(mine, axis=0, keepdims=True)
+        gfed8 = normalize_back(grad_summary, live["sc2"], live["inv2"], g01)
+        live["gfed8"] = gfed8
+        fed8_low = gfed8.astype(BF16)
+        live["fed8_low"] = fed8_low
+        active, slope = gelu_pair(mm(live["first8_low"], cols(UP, 0, 0, 768)))
+        live["act8"] = active.astype(BF16)
+        ga = mm_nt(fed8_low, cols(DOWN, 0, 0, 768))
+        live["gu8"] = (ga * slope).astype(BF16)
+        exchange(5, mm_nt(live["gu8"], cols(UP, 0, 0, 768)))
+
+    def cross_six():
+        part = exchange_sum(5)
+        for j in range(2):
+            GF[j * 128 : j * 128 + 1, :] = own_row(live["gfed8"], j)
+            ACC[j * 128 : j * 128 + 1, :] = own_row(part, j)
+
+    def norm_one_back():
+        def chunk(i, rows, carry):
+            gains, shifts = carry
+            grad = GF[rows, :] + ACC[rows, :]
+            scaled = SC1[rows, :]
+            att = normalize_back(grad, scaled, INV1[rows, 0:1], g00)
+            GF[rows, :] = att
+            FDL[rows, :] = att.astype(BF16)
+            return (
+                gains + jnp.sum(grad * scaled, axis=0, keepdims=True),
+                shifts + jnp.sum(grad, axis=0, keepdims=True),
+            )
+
+        zero = jnp.zeros((1, 768), F32)
+        gains, shifts = row_chunks(chunk, (zero, zero))
+        NV[0:1, :] = gains
+        NV[2:3, :] = shifts
+
+    def attn_backward(r, first):
+        GM[...] = mm(FDL[...], cols(ATT, r, 576, 192)).astype(BF16)
+
+        def segment(s, carry):
+            rows = pl.ds(pl.multiple_of(s * SEG, SEG), SEG)
+            qkv = QKV[r, rows, :]
+            gm = GM[rows, :]
+            gqs, gks, gvs = [], [], []
+            for h in range(3):
+                q = qkv[:, h * 64 : h * 64 + 64]
+                key = qkv[:, 192 + h * 64 : 256 + h * 64]
+                val = qkv[:, 384 + h * 64 : 448 + h * 64]
+                gmh = gm[:, h * 64 : h * 64 + 64]
+                prob = PR[r, h, rows, :]
+                gp = mm_nt(gmh, val)
+                inner = jnp.sum(gp * prob, axis=-1, keepdims=True)
+                gs = (prob * (gp - inner)).astype(BF16)
+                gqs.append(mm(gs, key) * SCALE)
+                gks.append(mm_tn(gs, q) * SCALE)
+                gvs.append(mm_tn(prob.astype(BF16), gmh))
+            GQ[rows, :] = jnp.concatenate(gqs + gks + gvs, axis=-1).astype(BF16)
+            return carry
+
+        lax.fori_loop(0, 2, segment, 0)
+        store_unit(
+            grad_unit(ATT, r),
+            [
+                (0, 576, lambda: mm(XT[...], GQ[...])),
+                (576, 192, lambda: mm(FDLT[...], MIX[r])),
+            ],
+        )
+        accumulate(first, mm_nt(GQ[...], cols(ATT, r, 0, 576)))
+
+    fac = {}
+
+    def factor_start():
+        wide = lambda v: v.astype(F32)
+        zero_a, zero_b = jnp.zeros((8, 192), F32), jnp.zeros((8, 576), F32)
+        att_left = jnp.concatenate([wide(live["xgqkv"]), zero_a], axis=-1)
+        att_right = jnp.concatenate([zero_b, wide(live["mix"])], axis=-1)
+        right = jnp.concatenate([wide(live["xact"]), wide(live["xgu"]), att_left, att_right], axis=0)
+        left = jnp.concatenate(
+            [wide(live["xfed_low"]), wide(live["xfirst_low"]), wide(live["summary_low"]), wide(live["xatt_low"])],
+            axis=0,
+        )
+        FAC[y, x, c, 0:32, :] = right.astype(BF16)
+        FAC[y, x, c, 32:64, :] = left.astype(BF16)
+        part = FAC.at[y, x, c]
+        fac[0] = remote(part, part, f_s.at[0], f_r.at[0], x_peer)
+
+    def factor_two():
+        fac[0].wait_recv()
+        part = FAC.at[y, :, c]
+        fac[1] = remote(part, part, f_s.at[1], f_r.at[1], y_peer)
+
+    def factor_three():
+        fac[1].wait_recv()
+        part = FAC.at[:, :, c]
+        fac[2] = remote(part, part, f_s.at[2], f_r.at[2], core_peer)
+
+    def turn_rows(value):
+        rows = value.shape[0]
+        full = jnp.concatenate([value, jnp.zeros((128 - rows, value.shape[1]), F32)], axis=0)
+        return full.T[:, 0:rows]
+
+    def write_unit(layer, k, value):
+        if k == ATT:
+            for i in range(3):
+                qkvg_ref[layer, i] = value[:, i * 192 : i * 192 + 192]
+            outg_ref[layer] = turn_rows(value[:, 576:768])
+        elif k == UP:
+            upg_ref[layer] = value
+        else:
+            downg_ref[layer] = turn_rows(value)
+
+    def factor_final():
+        fac[2].wait_recv()
+        left = FAC[:, :, :, 32:64, :].reshape(256, 768)
+        for i in range(2):
+            LT[:, i * 128 : i * 128 + 128] = left[i * 128 : i * 128 + 128, :].T
+        mine = LT[pl.ds(pl.multiple_of(dp * BLK, BLK), BLK), :].astype(F32)
+        kind = (lax.broadcasted_iota(jnp.int32, (BLK, 256), 1) // 8) % 4
+        right = FAC[:, :, :, 0:32, :].reshape(256, 768)
+        write_unit(1, DOWN, mm(jnp.where(kind == 0, mine, 0.0).astype(BF16), right))
+        write_unit(1, UP, mm(jnp.where(kind == 1, mine, 0.0).astype(BF16), right))
+        write_unit(1, ATT, mm(jnp.where(kind >= 2, mine, 0.0).astype(BF16), right))
+
+    vec = {}
+
+    def norm_grads_start():
+        exchange(6, NV[...])
+
+    def norm_grads_two():
+        total = jnp.where(row_of < 4, exchange_sum(6), NV[...])
+        pad = jnp.zeros((8, 32), F32)
+        for p in range(8):
+            SV[p // 4, (p // 2) % 2, p % 2] = jnp.concatenate([total[:, p * BLK : p * BLK + BLK], pad], axis=-1)
+        for m in range(1, 8):
+            ty = y if m // 4 == 0 else ny
+            tx = x if (m // 2) % 2 == 0 else nx
+            tc = c if m % 2 == 0 else nc
+            vec[m] = remote(
+                SV.at[ty, tx, tc], RSV.at[m - 1], v_s.at[m - 1], v_r.at[m - 1], (plane_index(m), z)
+            )
+
+    def norm_grads_final():
+        total = SV[y, x, c]
+        for m in range(1, 8):
+            vec[m].wait_recv()
+            total = total + RSV[m - 1]
+        gaing_ref[...] = total[0:2, 0:BLK]
+        shiftg_ref[...] = total[2:4, 0:BLK]
+        crossg_ref[0] = total[4:6, 0:BLK]
+        crossg_ref[1] = total[6:8, 0:BLK]
+
+    def eight_turned(dst, value):
+        full = jnp.concatenate([value.astype(F32), jnp.zeros((120, 768), F32)], axis=0)
+        dst[...] = full.T.astype(BF16)
+
+    def eight_rows(dst, value):
+        dst[...] = jnp.concatenate([value.astype(F32), jnp.zeros((120, 768), F32)], axis=0).astype(BF16)
+
+    cross_one()
+    ffn_back_one(1)
+    store_ffn(DOWN, 1, FDLT, ACT.at[1])
+    sum_start(0)
+    store_ffn(UP, 1, FLT, GU)
+    sum_start(1)
+    ffn_back_two(1, True)
+    cross_two()
+    pump(0)
+    ffn_back_one(2)
+    store_ffn(DOWN, 2, FDLT, ACT.at[2])
+    sum_start(2)
+    store_ffn(UP, 2, FLT, GU)
+    sum_start(3)
+    ffn_back_two(2, False)
+    cross_three()
+    pump(1)
+    ffn_back_one(3)
+    store_ffn(DOWN, 3, FDLT, ACT.at[3])
+    sum_start(4)
+    store_ffn(UP, 3, FLT, GU)
+    sum_start(5)
+    ffn_back_two(3, False)
+    cross_four()
+    factor_start()
+    pump(2)
+    cross_five()
+    pump(3)
+    ffn_back_one(0)
+    eight_turned(EL, live["fed8_low"])
+    eight_rows(ER, live["act8"])
+    store_ffn(DOWN, 0, FDLT, ACT.at[0], (EL, ER))
+    sum_start(6)
+    eight_turned(EL, live["first8_low"])
+    eight_rows(ER, live["gu8"])
+    store_ffn(UP, 0, FLT, GU, (EL, ER))
+    sum_start(7)
+    ffn_back_two(0, False)
+    cross_six()
+    norm_one_back()
+    norm_grads_start()
+    transpose_into(FDLT, FDL)
+    for table in (a1, b1, a2, b2, cc):
+        for i in range(9):
+            table[i].wait_send()
+            waited.append(id(table[i]))
+    pump(4)
+    factor_two()
+    attn_backward(1, True)
+    sum_start(8)
+    pump(5)
+    factor_three()
+    norm_grads_two()
+    attn_backward(2, False)
+    sum_start(9)
+    pump(6)
+    attn_backward(3, False)
+    sum_start(10)
+    pump(7)
+    attn_backward(0, False)
+    sum_start(11)
+    ing_ref[0] = (GF[...] + ACC[...]).astype(BF16)
+    pump(8)
+    factor_final()
+    pump(9)
+    norm_grads_final()
+    pump(10)
+    write_unit(0, DOWN, sum_final(DOWN))
+    pump(11)
+    write_unit(0, UP, sum_final(UP))
+    pump(12)
+    pump(13)
+    write_unit(0, ATT, sum_final(ATT))
+    for copy in sends:
+        if id(copy) not in waited:
+            copy.wait_send()
+
+
+def fused_body(
+    inputs, doc_ids, qkv_weight, out_weight, up_weight, down_weight, norm_gain, norm_shift, cotangent
+):
+    qkv_rows = qkv_weight.transpose(0, 2, 1, 3).reshape(2, 768, 576)
+    wa = jnp.concatenate([qkv_rows, out_weight.transpose(0, 2, 1)], axis=-1).reshape(2, 2, 2, 2, BLK, 768)
+    wu = up_weight.reshape(2, 2, 2, 2, BLK, 768)
+    wd = down_weight.reshape(2, 2, 2, 2, BLK, 768)
+    same = doc_ids[0][:, None] == doc_ids[0][None, :]
+    allowed = jnp.pad(same.astype(F32), ((0, 0), (0, 120)))
+    whole = pl.BlockSpec(memory_space=pl.ANY)
+    vmem = pl.BlockSpec(memory_space=pltpu.VMEM)
+    blocks = (2, 2, 2, BLK, 768)
+    sem = pltpu.SemaphoreType.DMA
+    return pl.pallas_call(
+        fused_kernel,
+        out_shape=(
+            jax.ShapeDtypeStruct((1, 256, 768), BF16),
+            jax.ShapeDtypeStruct((1, 256, 768), BF16),
+            jax.ShapeDtypeStruct((2, 3, BLK, 192), F32),
+            jax.ShapeDtypeStruct((2, 192, BLK), F32),
+            jax.ShapeDtypeStruct((2, BLK, 768), F32),
+            jax.ShapeDtypeStruct((2, 768, BLK), F32),
+            jax.ShapeDtypeStruct((2, BLK), F32),
+            jax.ShapeDtypeStruct((2, BLK), F32),
+            jax.ShapeDtypeStruct((2, 2, BLK), F32),
+        ),
+        in_specs=[whole, whole, whole, vmem, whole, whole, whole, vmem, vmem],
+        out_specs=(vmem,) * 9,
+        scratch_shapes=[
+            pltpu.VMEM((3, 4) + blocks, BF16),
+            pltpu.VMEM((2, 4) + blocks, BF16),
+            pltpu.VMEM((12, 2, 2, BLK, 768), BF16),
+            pltpu.VMEM((12, 2, HALF, 768), BF16),
+            pltpu.VMEM((12, 2, HALF, 768), BF16),
+            pltpu.VMEM((12, HALF, 768), BF16),
+            pltpu.VMEM((12, HALF, 768), BF16),
+            pltpu.VMEM((3, 3, BLK, 768), BF16),
+            pltpu.VMEM((3,) + blocks, BF16),
+            pltpu.VMEM((256, 768), BF16),
+            pltpu.VMEM((256, 768), BF16),
+            pltpu.VMEM((4, 256, 576), BF16),
+            pltpu.VMEM((4, 3, 256, 128), F32),
+            pltpu.VMEM((4, 256, 192), BF16),
+            pltpu.VMEM((4, 256, 768), BF16),
+            pltpu.VMEM((4, 256, 768), BF16),
+            pltpu.VMEM((256, 768), BF16),
+            pltpu.VMEM((256, 576), BF16),
+            pltpu.VMEM((256, 768), F32),
+            pltpu.VMEM((256, 768), F32),
+            pltpu.VMEM((256, 768), F32),
+            pltpu.VMEM((256, 768), F32),
+            pltpu.VMEM((256, 768), BF16),
+            pltpu.VMEM((768, 256), BF16),
+            pltpu.VMEM((256, 768), BF16),
+            pltpu.VMEM((768, 256), BF16),
+            pltpu.VMEM((768, 256), BF16),
+            pltpu.VMEM((256, 192), BF16),
+            pltpu.VMEM((8, 16, 768), BF16),
+            pltpu.VMEM((256, 128), F32),
+            pltpu.VMEM((256, 128), F32),
+            pltpu.VMEM((2, 2, 2, 64, 768), BF16),
+            pltpu.VMEM((768, 256), BF16),
+            pltpu.VMEM((768, 128), BF16),
+            pltpu.VMEM((128, 768), BF16),
+            pltpu.VMEM((7, 4, 8, 768), F32),
+            pltpu.VMEM((8, 768), F32),
+            pltpu.VMEM((2, 2, 2, 8, 128), F32),
+            pltpu.VMEM((7, 8, 128), F32),
+            sem((9,)),
+            sem((6, 9)),
+            sem((6, 9)),
+            sem((6, 12)),
+            sem((6, 12)),
+            sem((7, 3)),
+            sem((7, 3)),
+            sem((3,)),
+            sem((3,)),
+            sem((7,)),
+            sem((7,)),
+        ],
+        compiler_params=pltpu.CompilerParams(
+            collective_id=0, has_side_effects=True, vmem_limit_bytes=63 * 2**20
+        ),
+    )(
+        inputs, cotangent, cotangent.reshape(8, SEG, 768), allowed, wa, wu, wd, norm_gain, norm_shift
+    )
+
+
 def solution(mesh):
     in_specs = (
         P("dp", None, None),
@@ -297,4 +1123,6 @@
         P(None, "dp"),
         P(None, None, "dp"),
     )
-    return jax.shard_map(body, mesh=mesh, in_specs=in_specs, out_specs=out_specs, check_vma=False)
+    fits = dict(mesh.shape) == {"dp": 8, "tensor": 4}
+    chosen = fused_body if fits else body
+    return jax.shard_map(chosen, mesh=mesh, in_specs=in_specs, out_specs=out_specs, check_vma=False)

time: 826 us -> 179 us (0.22); the launches traced: 816 us -> 179 us
  waiting for transfers between devices: 520 us -> 0 us
  Pallas kernels: 0 us -> 150 us
  blocking collectives: 71.4 us -> 0 us
  local copies, waits for them, and re-layouts: 93.7 us -> 22.7 us
  matrix products: 56.3 us -> 0 us
  other arithmetic: 57.4 us -> 4.91 us
  between operations: 16 us -> 0.71 us
    psum x4 -> x0, waiting for transfers between devices: 263 us -> none  [the longest x2 136 us: forward_sum(): lax.psum(partial_term.astype(jnp.bfloat16), 'tensor').astype(jnp.float32)]
    unnamed x17 -> x0, waiting for transfers between devices: 201 us -> none
    pallas_call x0 -> x1, Pallas kernels: none -> 150 us  [fused_body(): pl.pallas_call(fused_kernel, out_shape=(jax.ShapeDtypeStruct((1, 256, 768...]
    psum x4 -> x0, blocking collectives: 71.4 us -> none  [the longest x2 35.7 us: cross_sum(): lax.psum(partial_term.astype(jnp.bfloat16), 'tensor').astype(jnp.float32)]
    dot_general x36 -> x0, matrix products: 56.3 us -> none  [the longest x2 7.41 us: expand_backward(): jnp.einsum('brf,brd->fd', active, grad_low, preferred_element_type=jnp.fl...]
    reduce_scatter x1 -> x0, waiting for transfers between devices: 55.4 us -> none  [body(): lax.psum_scatter(up_all, 'dp', scatter_dimension=1, tiled=True)]
    unnamed x175 -> x22, local copies, waits for them, and re-layouts: 57.8 us -> 6.55 us
    another operation x18 -> x0, local copies, waits for them, and re-layouts: 22.8 us -> none  [the longest x1 8.22 us: body(): down_all = jnp.stack([down_seg, down_cross])]
  transfers between devices with their start and end apart: 11 -> 0, of which waited for: 9 -> 0; matrix products, arithmetic and copies ran while one was open for 12% -> 0% of each run, Pallas kernels for 0% -> 0%
where the time goes in v1:
time: 179 us
  Pallas kernels  150 us (84%)
  local copies, waits for them, and re-layouts  22.7 us (13%)
  other arithmetic  4.91 us (3%)
    pallas_call x1, Pallas kernels, fused_body(): pl.pallas_call(fused_kernel, out_shape=(jax.ShapeDtypeStruct((1, 256, 768...  150 us
    concatenate x2, local copies, waits for them, and re-layouts, fused_body(): jnp.concatenate([qkv_rows, out_weight.transpose(0, 2, 1)], axis=-1)  12.5 us
    unnamed x22, local copies, waits for them, and re-layouts  6.55 us

profile of v1, /device:TPU:0, one launch (start us, length us, event | category | flops | bytes accessed | tf_op | source)
XLA Modules:
  0.0 178.5 jit_solution(15916950424798021733)
XLA Ops:
  0.6 0.8 broadcast_compare_fusion
  1.4 0.6 pad_convert_fusion.allowed_ref
  2.0 1.3 copy.21
  3.4 7.7 %concatenate.8 = bf16[2,2,2,2,96,576]{4,3,2,1,5,0:T(2,128)(2,1)S(1)} reshape(bf16[2,768,3,192]{1,3,2,0:T(8,128)(2,1)} %bitcast.15) | data formatting | bytes 3538944 | tf_op jit(solution)/shard_map/concatenate | solution.py:1019
  11.1 4.8 %copy.22 = bf16[2,2,2,2,96,576]{5,4,3,2,1,0:T(8,128)(2,1)} copy(bf16[2,2,2,2,96,576]{4,3,2,1,5,0:T(2,128)(2,1)S(1)} %concatenate.8) | data formatting | bytes 3538944 | tf_op jit(solution)/shard_map/concatenate | solution.py:1019
  15.9 3.5 %pad_maximum_fusion.wa_hbm = bf16[2,2,2,2,96,768]{5,4,3,2,1,0:T(8,128)(2,1)} fusion(bf16[2,2,2,2,96,192]{5,4,3,2,1,0:T(8,128)(2,1)S(1)} %bitcast.12, bf16[2,2,2,2,96,576]{5,4,3,2,1,0:T(8,128)(2,1)} %copy.22), kind=kLoop, calls=%fused_computation | loop fusion | flops 4718592 | bytes 4718592 | tf_op jit(solution)/shard_map/concatenate | solution.py:1019
  19.4 150.2 %shard_map.160 = (bf16[1,256,768]{2,1,0:T(8,128)(2,1)}, bf16[1,256,768]{2,1,0:T(8,128)(2,1)}, f32[2,3,96,192]{3,2,1,0:T(8,128)}, f32[2,192,96]{2,1,0:T(8,128)}, ...) custom-call(bf16[1,1024,768]{2,1,0:T(8,128)(2,1)} %tokens_hbm.1, ...), custom_call_target="tpu_custom_call" | custom-call | tf_op jit(solution)/shard_map/pallas_call | solution.py:1028
  169.6 0.0 copy-start.2
  169.6 0.0 copy-start.1
  169.6 0.0 copy-start.3
  169.6 0.0 copy-start
  169.6 2.3 %copy.23 = f32[2,768,96]{1,2,0:T(8,128)} copy(f32[2,768,96]{2,1,0:T(8,128)} %get-tuple-element.23) | data formatting | bytes 1179648 | tf_op jit(solution)/shard_map/pallas_call | solution.py:1028
  172.0 0.0 copy-start.6
  172.0 0.0 copy-start.5
  172.0 0.0 copy-start.4
  172.0 1.8 copy.32
  173.7 0.0 copy-done.2
  173.7 0.7 copy.33
  174.5 0.0 copy-done.1
  174.5 0.8 copy.34
  175.3 0.0 copy-done.3
  175.3 0.7 copy.35
  176.0 0.0 copy-done
  176.0 0.8 copy.36
  176.8 0.0 copy-done.6
  176.8 0.6 copy.37
  177.4 0.0 copy-done.5
  177.4 0.6 copy.38
  177.9 0.0 copy-done.4
  177.9 0.6 copy.39
Async XLA Ops:
  169.6 4.2 %copy-start.2 = (bf16[1,256,768]{2,1,0:T(8,128)(2,1)S(1)}, bf16[1,256,768]{2,1,0:T(8,128)(2,1)}, u32[]{:S(2)}) copy-start(bf16[1,256,768]{2,1,0:T(8,128)(2,1)} %get-tuple-element.37) | copy-start | bytes 1179652
  169.6 4.9 %copy-start.1 = (f32[2,3,96,192]{3,2,1,0:T(8,128)S(1)}, f32[2,3,96,192]{3,2,1,0:T(8,128)}, u32[]{:S(2)}) copy-start(f32[2,3,96,192]{3,2,1,0:T(8,128)} %get-tuple-element.38) | copy-start | bytes 1327108
  169.6 5.7 %copy-start.3 = (f32[2,192,96]{2,1,0:T(8,128)S(1)}, f32[2,192,96]{2,1,0:T(8,128)}, u32[]{:S(2)}) copy-start(f32[2,192,96]{2,1,0:T(8,128)} %get-tuple-element.39) | copy-start | bytes 442372
  169.6 6.4 %copy-start = (f32[2,96,768]{2,1,0:T(8,128)S(1)}, f32[2,96,768]{2,1,0:T(8,128)}, u32[]{:S(2)}) copy-start(f32[2,96,768]{2,1,0:T(8,128)} %get-tuple-element.40) | copy-start | bytes 1769476
  172.0 4.8 %copy-start.6 = (f32[2,96]{1,0:T(2,128)S(1)}, f32[2,96]{1,0:T(2,128)}, u32[]{:S(2)}) copy-start(f32[2,96]{1,0:T(2,128)} %get-tuple-element.42) | copy-start | bytes 2308
  172.0 5.4 %copy-start.5 = (f32[2,96]{1,0:T(2,128)S(1)}, f32[2,96]{1,0:T(2,128)}, u32[]{:S(2)}) copy-start(f32[2,96]{1,0:T(2,128)} %get-tuple-element.43) | copy-start | bytes 2308
  172.0 6.0 %copy-start.4 = (f32[2,2,96]{2,1,0:T(2,128)S(1)}, f32[2,2,96]{2,1,0:T(2,128)}, u32[]{:S(2)}) copy-start(f32[2,2,96]{2,1,0:T(2,128)} %get-tuple-element.44) | copy-start | bytes 4612

commit v2 on v1

--- a/solution.py
+++ b/solution.py
@@ -319,7 +319,7 @@
 
 
 def fused_kernel(
-    tokens_hbm, cot_hbm, cot_seg, allowed_ref, wa_hbm, wu_hbm, wd_hbm, gain_ref, shift_ref,
+    tokens_hbm, cot_hbm, cot_seg, doc_ref, wq_hbm, wo_hbm, wu_hbm, wd_hbm, gain_ref, shift_ref,
     out_ref, ing_ref, qkvg_ref, outg_ref, upg_ref, downg_ref, gaing_ref, shiftg_ref, crossg_ref,
     W, G, RC, RA1, RB1, RA2, RB2, RZ, L1, X, COT, QKV, PR, MIX, ACT, DG, GU, GQ, ACC, SC1, SC2, GF,
     FL, FLT, FDL, FDLT, XT, GM, C8, INV1, INV2, FAC, LT, EL, ER, E, NV, SV, RSV,
@@ -362,11 +362,15 @@
         loads[name] = copy
 
     load("x", 0, tokens_hbm.at[0, pl.ds(pl.multiple_of(z * 256, 256), 256)], X)
-    load("wa", 1, wa_hbm.at[0], W.at[ATT, 0])
+    load("wqk", 1, wq_hbm.at[0, pl.ds(0, 2)], W.at[ATT, 0, 0])
+    load("wv", 9, wq_hbm.at[0, 2], W.at[ATT, 0, 1, 0])
+    load("wo", 10, wo_hbm.at[0], W.at[ATT, 0, 1, 1])
     load("wu", 2, wu_hbm.at[0], W.at[UP, 0])
     load("wd", 3, wd_hbm.at[0], W.at[DOWN, 0])
     load("cot", 4, cot_hbm.at[0, pl.ds(pl.multiple_of(z * 256, 256), 256)], COT)
-    load("l1a", 5, wa_hbm.at[1], L1.at[ATT])
+    load("l1qk", 5, wq_hbm.at[1, pl.ds(0, 2)], L1.at[ATT, 0])
+    load("l1v", 11, wq_hbm.at[1, 2], L1.at[ATT, 1, 0])
+    load("l1o", 12, wo_hbm.at[1], L1.at[ATT, 1, 1])
     load("l1u", 6, wu_hbm.at[1], L1.at[UP])
     load("l1d", 7, wd_hbm.at[1], L1.at[DOWN])
     load("c8", 8, cot_seg.at[:, pl.ds(0, 16)], C8)
@@ -378,12 +382,14 @@
         pl.semaphore_signal(barrier, inc=1, device_id=z_peer[r], device_id_type=MESH)
     pl.semaphore_wait(barrier, 10)
 
-    own_hbm = [wa_hbm.at[0], wu_hbm.at[0], wd_hbm.at[0]]
+    own_unit = [W.at[ATT, 0], wu_hbm.at[0], wd_hbm.at[0]]
     units = [(ATT, 1), (ATT, 2), (ATT, 3), (UP, 1), (DOWN, 1), (UP, 2), (DOWN, 2), (UP, 3), (DOWN, 3)]
     zc, a1, b1, a2, b2, cc = {}, {}, {}, {}, {}, {}
+    for name in ("wqk", "wv", "wo"):
+        loads[name].wait()
     for i, (k, r) in enumerate(units):
         zc[i] = remote(
-            own_hbm[k].at[y, x, c], W.at[k, r, y, x, c], ag_s.at[0, i], ag_r.at[0, i], z_peer[r]
+            own_unit[k].at[y, x, c], W.at[k, r, y, x, c], ag_s.at[0, i], ag_r.at[0, i], z_peer[r]
         )
 
     def gather_tick(t):
@@ -421,6 +427,12 @@
     def cols(k, r, start, size):
         return unit_value(W.at[k, r, :, :, :, :, pl.ds(start, size)])
 
+    def qkv_rows(ref):
+        return jnp.concatenate([ref[0].reshape(384, 768), ref[1, 0].reshape(192, 768)], axis=0)
+
+    def out_rows(ref):
+        return ref[1, 1].reshape(192, 768)
+
     def accumulate(first, value):
         if first:
             ACC[...] = value
@@ -428,7 +440,7 @@
             ACC[...] += value
 
     def attn_forward(r):
-        QKV[r] = mm(X[...], cols(ATT, r, 0, 576)).astype(BF16)
+        QKV[r] = mm_nt(X[...], qkv_rows(W.at[ATT, r])).astype(BF16)
 
         def segment(s, carry):
             rows = pl.ds(pl.multiple_of(s * SEG, SEG), SEG)
@@ -448,7 +460,7 @@
             return carry
 
         lax.fori_loop(0, 2, segment, 0)
-        accumulate(r == 0, mm_nt(MIX[r], cols(ATT, r, 576, 192)))
+        accumulate(r == 0, mm(MIX[r], out_rows(W.at[ATT, r])))
 
     def row_chunks(body, init=0):
         def one(i, carry):
@@ -501,7 +513,6 @@
             dst[:, i * 128 : i * 128 + 128] = src[i * 128 : i * 128 + 128, :].T
 
     loads["x"].wait()
-    loads["wa"].wait()
     attn_forward(0)
     gather_tick(0)
     gather_tick(1)
@@ -701,10 +712,14 @@
         live["summary"] = summary
         live["summary_low"] = summary.astype(BF16)
         live["first8_low"] = first8.astype(BF16)
-        loads["l1a"].wait()
-        qkv = mm(live["summary_low"], l1(ATT, 0, 576)).astype(BF16).astype(F32)
+        for name in ("l1qk", "l1v", "l1o"):
+            loads[name].wait()
+        qkv = mm_nt(live["summary_low"], qkv_rows(L1.at[ATT])).astype(BF16).astype(F32)
         pad = jnp.zeros((120, 64), F32)
-        keep = allowed_ref[...] > 0.5
+        ids = jnp.broadcast_to(doc_ref[...].astype(F32), (8, 8))
+        eye = lax.broadcasted_iota(jnp.int32, (8, 8), 0) == lax.broadcasted_iota(jnp.int32, (8, 8), 1)
+        same = ids == jnp.sum(jnp.where(eye, ids, 0.0), axis=1, keepdims=True)
+        keep = jnp.concatenate([jnp.where(same, 1.0, 0.0), jnp.zeros((8, 120), F32)], axis=1) > 0.5
         mixes = []
         for h in range(3):
             q = qkv[:, h * 64 : h * 64 + 64].astype(BF16)
@@ -718,7 +733,7 @@
             mixes.append(mm(prob.astype(BF16), val))
         mix = jnp.concatenate(mixes, axis=-1).astype(BF16)
         live["mix"] = mix
-        exchange(1, mm_nt(mix, l1(ATT, 576, 192)))
+        exchange(1, mm(mix, out_rows(L1.at[ATT])))
 
     def cross_two():
         attended = exchange_sum(1)
@@ -758,7 +773,7 @@
         live["xga"] = grad_att
         att_low = grad_att.astype(BF16)
         live["xatt_low"] = att_low
-        gm = mm(att_low, l1(ATT, 576, 192)).astype(BF16)
+        gm = mm_nt(att_low, out_rows(L1.at[ATT])).astype(BF16)
         gqs, gks, gvs = [], [], []
         for h in range(3):
             gmh = gm[:, h * 64 : h * 64 + 64]
@@ -771,7 +786,7 @@
             gvs.append(mm_tn(prob.astype(BF16), gmh)[0:8, :])
         gqkv = jnp.concatenate(gqs + gks + gvs, axis=-1).astype(BF16)
         live["xgqkv"] = gqkv
-        exchange(4, mm_nt(gqkv, l1(ATT, 0, 576)))
+        exchange(4, mm(gqkv, qkv_rows(L1.at[ATT])))
 
     def cross_five():
         grad_summary = live["xga"] + exchange_sum(4)
@@ -813,7 +828,7 @@
         NV[2:3, :] = shifts
 
     def attn_backward(r, first):
-        GM[...] = mm(FDL[...], cols(ATT, r, 576, 192)).astype(BF16)
+        GM[...] = mm_nt(FDL[...], out_rows(W.at[ATT, r])).astype(BF16)
 
         def segment(s, carry):
             rows = pl.ds(pl.multiple_of(s * SEG, SEG), SEG)
@@ -843,7 +858,7 @@
                 (576, 192, lambda: mm(FDLT[...], MIX[r])),
             ],
         )
-        accumulate(first, mm_nt(GQ[...], cols(ATT, r, 0, 576)))
+        accumulate(first, mm(GQ[...], qkv_rows(W.at[ATT, r])))
 
     fac = {}
 
@@ -885,7 +900,7 @@
         elif k == UP:
             upg_ref[layer] = value
         else:
-            downg_ref[layer] = turn_rows(value)
+            downg_ref[layer] = value
 
     def factor_final():
         fac[2].wait_recv()
@@ -1012,20 +1027,31 @@
             copy.wait_send()
 
 
+def settle_kernel(*refs):
+    sources, targets, held, sems = refs[:9], refs[9:18], refs[18:27], refs[27]
+    arrive = [pltpu.make_async_copy(sources[i], held[i], sems.at[0, i]) for i in range(9)]
+    leave = [pltpu.make_async_copy(held[i], targets[i], sems.at[1, i]) for i in range(9)]
+    for copy in arrive:
+        copy.start()
+    for i in range(9):
+        arrive[i].wait()
+        leave[i].start()
+    for copy in leave:
+        copy.wait()
+
+
 def fused_body(
     inputs, doc_ids, qkv_weight, out_weight, up_weight, down_weight, norm_gain, norm_shift, cotangent
 ):
-    qkv_rows = qkv_weight.transpose(0, 2, 1, 3).reshape(2, 768, 576)
-    wa = jnp.concatenate([qkv_rows, out_weight.transpose(0, 2, 1)], axis=-1).reshape(2, 2, 2, 2, BLK, 768)
+    wq = qkv_weight.swapaxes(2, 3).reshape(2, 3, 2, BLK, 768)
+    wo = out_weight.reshape(2, 2, BLK, 768)
     wu = up_weight.reshape(2, 2, 2, 2, BLK, 768)
     wd = down_weight.reshape(2, 2, 2, 2, BLK, 768)
-    same = doc_ids[0][:, None] == doc_ids[0][None, :]
-    allowed = jnp.pad(same.astype(F32), ((0, 0), (0, 120)))
     whole = pl.BlockSpec(memory_space=pl.ANY)
     vmem = pl.BlockSpec(memory_space=pltpu.VMEM)
     blocks = (2, 2, 2, BLK, 768)
     sem = pltpu.SemaphoreType.DMA
-    return pl.pallas_call(
+    results = pl.pallas_call(
         fused_kernel,
         out_shape=(
             jax.ShapeDtypeStruct((1, 256, 768), BF16),
@@ -1033,12 +1059,12 @@
             jax.ShapeDtypeStruct((2, 3, BLK, 192), F32),
             jax.ShapeDtypeStruct((2, 192, BLK), F32),
             jax.ShapeDtypeStruct((2, BLK, 768), F32),
-            jax.ShapeDtypeStruct((2, 768, BLK), F32),
+            jax.ShapeDtypeStruct((2, BLK, 768), F32),
             jax.ShapeDtypeStruct((2, BLK), F32),
             jax.ShapeDtypeStruct((2, BLK), F32),
             jax.ShapeDtypeStruct((2, 2, BLK), F32),
         ),
-        in_specs=[whole, whole, whole, vmem, whole, whole, whole, vmem, vmem],
+        in_specs=[whole, whole, whole, vmem, whole, whole, whole, whole, vmem, vmem],
         out_specs=(vmem,) * 9,
         scratch_shapes=[
             pltpu.VMEM((3, 4) + blocks, BF16),
@@ -1080,7 +1106,7 @@
             pltpu.VMEM((8, 768), F32),
             pltpu.VMEM((2, 2, 2, 8, 128), F32),
             pltpu.VMEM((7, 8, 128), F32),
-            sem((9,)),
+            sem((13,)),
             sem((6, 9)),
             sem((6, 9)),
             sem((6, 12)),
@@ -1096,8 +1122,16 @@
             collective_id=0, has_side_effects=True, vmem_limit_bytes=63 * 2**20
         ),
     )(
-        inputs, cotangent, cotangent.reshape(8, SEG, 768), allowed, wa, wu, wd, norm_gain, norm_shift
-    )
+        inputs, cotangent, cotangent.reshape(8, SEG, 768), doc_ids, wq, wo, wu, wd, norm_gain, norm_shift
+    )
+    final = pl.pallas_call(
+        settle_kernel,
+        out_shape=tuple(jax.ShapeDtypeStruct(v.shape, v.dtype) for v in results),
+        in_specs=[whole] * 9,
+        out_specs=(whole,) * 9,
+        scratch_shapes=[pltpu.VMEM(v.shape, v.dtype) for v in results] + [sem((2, 9))],
+    )(*results)
+    return final[:5] + (final[5].swapaxes(1, 2),) + final[6:]
 
 
 def solution(mesh):

time: 179 us -> 154 us (0.86)
  local copies, waits for them, and re-layouts: 22.7 us -> 0 us
  other arithmetic: 4.91 us -> 0 us
  Pallas kernels: 150 us -> 152 us
    concatenate x2 -> x0, local copies, waits for them, and re-layouts: 12.5 us -> none  [fused_body(): jnp.concatenate([qkv_rows, out_weight.transpose(0, 2, 1)], axis=-1)]
    unnamed x22 -> x0, local copies, waits for them, and re-layouts: 6.55 us -> none
    concatenate x1 -> x0, other arithmetic: 3.51 us -> none  [fused_body(): jnp.concatenate([qkv_rows, out_weight.transpose(0, 2, 1)], axis=-1)]
    pallas_call x0 -> x1, Pallas kernels: none -> 2.74 us  [fused_body(): pl.pallas_call(settle_kernel, out_shape=tuple((jax.ShapeDtypeStruct(v.sha...]
    pallas_call x1 -> x0, local copies, waits for them, and re-layouts: 2.33 us -> none  [fused_body(): pl.pallas_call(fused_kernel, out_shape=(jax.ShapeDtypeStruct((1, 256, 768...]
where the time goes in v2:
time: 154 us; the launch traced here: 153 us
  Pallas kernels  152 us (99%)
    pallas_call x1, Pallas kernels, fused_body(): pl.pallas_call(fused_kernel, out_shape=(jax.ShapeDtypeStruct((1, 256, 768...  150 us

profile of v2, /device:TPU:0, one launch (start us, length us, event | category | flops | bytes accessed | tf_op | source)
XLA Modules:
  0.0 153.2 jit_solution(1377714578924065215)
XLA Ops:
  0.6 149.7 %shard_map.160 = (bf16[1,256,768]{2,1,0:T(8,128)(2,1)}, bf16[1,256,768]{2,1,0:T(8,128)(2,1)}, f32[2,3,96,192]{3,2,1,0:T(8,128)}, f32[2,192,96]{2,1,0:T(8,128)}, ...) custom-call(bf16[1,1024,768]{2,1,0:T(8,128)(2,1)} %tokens_hbm.1, ...), custom_call_target="tpu_custom_call" | custom-call | tf_op jit(solution)/shard_map/pallas_call | solution.py:1054
  150.3 2.7 %shard_map.161 = (bf16[1,256,768]{2,1,0:T(8,128)(2,1)}, bf16[1,256,768]{2,1,0:T(8,128)(2,1)}, f32[2,3,96,192]{3,2,1,0:T(8,128)}, f32[2,192,96]{2,1,0:T(8,128)}, ...) custom-call(bf16[1,256,768]{2,1,0:T(8,128)(2,1)} %get-tuple-element., ...), custom_call_target="tpu_custom_call" | custom-call | tf_op jit(solution)/shard_map/pallas_call | solution.py:1127

commit v3 on v2

--- a/solution.py
+++ b/solution.py
@@ -321,9 +321,9 @@
 def fused_kernel(
     tokens_hbm, cot_hbm, cot_seg, doc_ref, wq_hbm, wo_hbm, wu_hbm, wd_hbm, gain_ref, shift_ref,
     out_ref, ing_ref, qkvg_ref, outg_ref, upg_ref, downg_ref, gaing_ref, shiftg_ref, crossg_ref,
-    W, G, RC, RA1, RB1, RA2, RB2, RZ, L1, X, COT, QKV, PR, MIX, ACT, DG, GU, GQ, ACC, SC1, SC2, GF,
-    FL, FLT, FDL, FDLT, XT, GM, C8, INV1, INV2, FAC, LT, EL, ER, E, NV, SV, RSV,
-    sem_local, ag_s, ag_r, rs_s, rs_r, e_s, e_r, f_s, f_r, v_s, v_r,
+    W, G, RC, RA1, RB1, RA2, RB2, RZ, L1, XA, COT, QKV, PR, MIX, ACT, DG, GU, GQ, ACC, SC1, SC2, GF,
+    FL, FLT, FDL, FDLT, XT, GM, C8, INV1, INV2, FAC, LT, GS, E, NV, SV, RSV,
+    sem_local, zg_s, zg_r, ag_s, ag_r, rs_s, rs_r, e_s, e_r, f_s, f_r, v_s, v_r,
 ):
     dp = lax.axis_index("dp")
     z = lax.axis_index("tensor")
@@ -334,6 +334,7 @@
     core_peer = (dp + 1 - 2 * c, z)
     x_peer = (dp + 2 - 4 * x, z)
     y_peer = (dp + 4 - 8 * y, z)
+    left_peer, right_peer = (dp, jnp.maximum(z - 1, 0)), (dp, jnp.minimum(z + 1, 3))
     z_peer = [None, (dp, z + 1 - 2 * (z % 2)), (dp, z + 2 - 4 * (z // 2)), (dp, 3 - z)]
     z_of = [z, z + 1 - 2 * (z % 2), z + 2 - 4 * (z // 2), 3 - z]
 
@@ -361,12 +362,12 @@
         copy.start()
         loads[name] = copy
 
-    load("x", 0, tokens_hbm.at[0, pl.ds(pl.multiple_of(z * 256, 256), 256)], X)
-    load("wqk", 1, wq_hbm.at[0, pl.ds(0, 2)], W.at[ATT, 0, 0])
-    load("wv", 9, wq_hbm.at[0, 2], W.at[ATT, 0, 1, 0])
-    load("wo", 10, wo_hbm.at[0], W.at[ATT, 0, 1, 1])
-    load("wu", 2, wu_hbm.at[0], W.at[UP, 0])
-    load("wd", 3, wd_hbm.at[0], W.at[DOWN, 0])
+    load("x", 0, tokens_hbm.at[0], XA)
+    load("wqk", 1, wq_hbm.at[0, pl.ds(0, 2)], W.at[ATT, z, 0])
+    load("wv", 9, wq_hbm.at[0, 2], W.at[ATT, z, 1, 0])
+    load("wo", 10, wo_hbm.at[0], W.at[ATT, z, 1, 1])
+    load("wu", 2, wu_hbm.at[0], W.at[UP, z])
+    load("wd", 3, wd_hbm.at[0], W.at[DOWN, z])
     load("cot", 4, cot_hbm.at[0, pl.ds(pl.multiple_of(z * 256, 256), 256)], COT)
     load("l1qk", 5, wq_hbm.at[1, pl.ds(0, 2)], L1.at[ATT, 0])
     load("l1v", 11, wq_hbm.at[1, 2], L1.at[ATT, 1, 0])
@@ -382,41 +383,72 @@
         pl.semaphore_signal(barrier, inc=1, device_id=z_peer[r], device_id_type=MESH)
     pl.semaphore_wait(barrier, 10)
 
-    own_unit = [W.at[ATT, 0], wu_hbm.at[0], wd_hbm.at[0]]
-    units = [(ATT, 1), (ATT, 2), (ATT, 3), (UP, 1), (DOWN, 1), (UP, 2), (DOWN, 2), (UP, 3), (DOWN, 3)]
-    zc, a1, b1, a2, b2, cc = {}, {}, {}, {}, {}, {}
-    for name in ("wqk", "wv", "wo"):
-        loads[name].wait()
-    for i, (k, r) in enumerate(units):
-        zc[i] = remote(
-            own_unit[k].at[y, x, c], W.at[k, r, y, x, c], ag_s.at[0, i], ag_r.at[0, i], z_peer[r]
+    own_unit = [W.at[ATT, z], wu_hbm.at[0], wd_hbm.at[0]]
+    units = [(k, r) for k in (ATT, UP, DOWN) for r in (1, 2, 3)]
+    a1, b1, a2, b2, cc = {}, {}, {}, {}, {}
+    passed = []
+
+    def z_copy(src, k, shard, side):
+        return pltpu.make_async_remote_copy(
+            src_ref=src,
+            dst_ref=W.at[k, shard, y, x, c],
+            send_sem=zg_s.at[k * 4 + shard, side],
+            recv_sem=zg_r.at[k * 4 + shard],
+            device_id=(left_peer, right_peer)[side],
+            device_id_type=MESH,
         )
+
+    def pass_on(condition, copy):
+        @pl.when(condition)
+        def _():
+            copy.start()
+
+        passed.append((condition, copy))
+
+    def z_own(k):
+        src = own_unit[k].at[y, x, c]
+        pass_on(z > 0, z_copy(src, k, z, 0))
+        pass_on(z < 3, z_copy(src, k, z, 1))
+
+    def z_step(k, step):
+        for side in range(2):
+            shard = z - 1 - step if side else z + 1 + step
+            there = shard >= 0 if side else shard <= 3
+            further = jnp.logical_and(there, z < 3 if side else z > 0)
+            shard = jnp.clip(shard, 0, 3)
+            copy = z_copy(W.at[k, shard, y, x, c], k, shard, side)
+
+            @pl.when(there)
+            def _():
+                copy.wait_recv()
+
+            pass_on(further, copy)
 
     def gather_tick(t):
         i = t
         if 0 <= i < 9:
             k, r = units[i]
-            zc[i].wait_recv()
-            part = W.at[k, r, y, x, c, pl.ds(0, HALF)]
-            a1[i] = remote(part, part, ag_s.at[1, i], ag_r.at[1, i], x_peer)
-            part = W.at[k, r, y, x, c, pl.ds(HALF, HALF)]
-            b1[i] = remote(part, part, ag_s.at[2, i], ag_r.at[2, i], y_peer)
+            z_step(k, r - 1)
+            part = W.at[k, z_of[r], y, x, c, pl.ds(0, HALF)]
+            a1[i] = remote(part, part, ag_s.at[0, i], ag_r.at[0, i], x_peer)
+            part = W.at[k, z_of[r], y, x, c, pl.ds(HALF, HALF)]
+            b1[i] = remote(part, part, ag_s.at[1, i], ag_r.at[1, i], y_peer)
         i = t - 1
         if 0 <= i < 9:
             k, r = units[i]
             a1[i].wait_recv()
-            part = W.at[k, r, y, :, c, pl.ds(0, HALF)]
-            a2[i] = remote(part, part, ag_s.at[3, i], ag_r.at[3, i], y_peer)
+            part = W.at[k, z_of[r], y, :, c, pl.ds(0, HALF)]
+            a2[i] = remote(part, part, ag_s.at[2, i], ag_r.at[2, i], y_peer)
             b1[i].wait_recv()
-            part = W.at[k, r, :, x, c, pl.ds(HALF, HALF)]
-            b2[i] = remote(part, part, ag_s.at[4, i], ag_r.at[4, i], x_peer)
+            part = W.at[k, z_of[r], :, x, c, pl.ds(HALF, HALF)]
+            b2[i] = remote(part, part, ag_s.at[3, i], ag_r.at[3, i], x_peer)
         i = t - 2
         if 0 <= i < 9:
             k, r = units[i]
             a2[i].wait_recv()
             b2[i].wait_recv()
-            part = W.at[k, r, :, :, c]
-            cc[i] = remote(part, part, ag_s.at[5, i], ag_r.at[5, i], core_peer)
+            part = W.at[k, z_of[r], :, :, c]
+            cc[i] = remote(part, part, ag_s.at[4, i], ag_r.at[4, i], core_peer)
         i = t - 3
         if 0 <= i < 9:
             cc[i].wait_recv()
@@ -425,7 +457,7 @@
         return ref[...].reshape(768, ref.shape[-1])
 
     def cols(k, r, start, size):
-        return unit_value(W.at[k, r, :, :, :, :, pl.ds(start, size)])
+        return unit_value(W.at[k, z_of[r], :, :, :, :, pl.ds(start, size)])
 
     def qkv_rows(ref):
         return jnp.concatenate([ref[0].reshape(384, 768), ref[1, 0].reshape(192, 768)], axis=0)
@@ -440,7 +472,7 @@
             ACC[...] += value
 
     def attn_forward(r):
-        QKV[r] = mm_nt(X[...], qkv_rows(W.at[ATT, r])).astype(BF16)
+        QKV[r] = mm_nt(XA[own_rows, :], qkv_rows(W.at[ATT, z_of[r]])).astype(BF16)
 
         def segment(s, carry):
             rows = pl.ds(pl.multiple_of(s * SEG, SEG), SEG)
@@ -460,7 +492,9 @@
             return carry
 
         lax.fori_loop(0, 2, segment, 0)
-        accumulate(r == 0, mm(MIX[r], out_rows(W.at[ATT, r])))
+        accumulate(r == 0, mm(MIX[r], out_rows(W.at[ATT, z_of[r]])))
+
+    own_rows = pl.ds(pl.multiple_of(z * 256, 256), 256)
 
     def row_chunks(body, init=0):
         def one(i, carry):
@@ -475,7 +509,8 @@
 
     def norm_one():
         def chunk(i, rows, carry):
-            scaled, inverse = normalize(X[rows, :].astype(F32) + ACC[rows, :])
+            mine = XA[pl.ds(pl.multiple_of(z * 256 + i * 64, 64), 64), :]
+            scaled, inverse = normalize(mine.astype(F32) + ACC[rows, :])
             SC1[rows, :] = scaled
             INV1[rows, :] = jnp.broadcast_to(inverse, (64, 128))
             FL[rows, :] = (scaled * g00 + b00).astype(BF16)
@@ -486,7 +521,7 @@
     def ffn_forward(r):
         def block(n, carry):
             part = pl.ds(pl.multiple_of(n * 256, 256), 256)
-            upward = mm(FL[...], unit_value(W.at[UP, r, :, :, :, :, part]))
+            upward = mm(FL[...], unit_value(W.at[UP, z_of[r], :, :, :, :, part]))
             active, slope = gelu_pair(upward)
             ACT[r, :, part] = active.astype(BF16)
             DG[r, :, part] = slope.astype(DG.dtype)
@@ -508,41 +543,9 @@
 
         row_chunks(chunk)
 
-    def transpose_into(dst, src):
+    def transpose_into(dst, src, start=0):
         for i in range(2):
-            dst[:, i * 128 : i * 128 + 128] = src[i * 128 : i * 128 + 128, :].T
-
-    loads["x"].wait()
-    attn_forward(0)
-    gather_tick(0)
-    gather_tick(1)
-    transpose_into(XT, X)
-    gather_tick(2)
-    gather_tick(3)
-    attn_forward(1)
-    gather_tick(4)
-    attn_forward(2)
-    gather_tick(5)
-    attn_forward(3)
-    norm_one()
-    loads["wu"].wait()
-    loads["wd"].wait()
-    gather_tick(6)
-    ffn_forward(0)
-    ffn_down(0)
-    gather_tick(7)
-    ffn_forward(1)
-    ffn_down(1)
-    gather_tick(8)
-    transpose_into(FLT, FL)
-    gather_tick(9)
-    ffn_forward(2)
-    ffn_down(2)
-    gather_tick(10)
-    ffn_forward(3)
-    gather_tick(11)
-    ffn_down(3)
-    norm_two()
+            dst[:, i * 128 : i * 128 + 128] = src[pl.ds(pl.multiple_of(start + i * 128, 128), 128), :].T
 
     exch = {}
 
@@ -562,32 +565,15 @@
     row_of = lax.broadcasted_iota(jnp.int32, (8, 768), 0)
     pair_of = row_of // 2
 
-    def assemble(e, start):
-        total = None
-        for r in range(4):
-            two = E[e, r][start : start + 2, :]
-            four = jnp.concatenate([two, two, two, two], axis=0)
-            part = jnp.where(pair_of == z_of[r], four, 0.0)
-            total = part if total is None else total + part
-        return total
-
     def own_row(value, j):
         return jnp.sum(jnp.where(row_of == 2 * z + j, value, 0.0), axis=0, keepdims=True)
 
-    def two_rows(ref):
-        return jnp.concatenate([ref[0:1, :], ref[128:129, :]], axis=0)
-
-    inv_two = jnp.broadcast_to(two_rows(INV2)[:, 0:1], (2, 768))
-    first_two = two_rows(SC1) * g00 + b00
-    exchange(0, jnp.concatenate([two_rows(SC2), first_two, inv_two, inv_two], axis=0))
-
-    loads["cot"].wait()
 
     def norm_two_back():
         def chunk(i, rows, carry):
             gains, shifts = carry
             which = lax.broadcasted_iota(jnp.int32, (64, 768), 0) + i * 64
-            grad = jnp.where(which % SEG == 0, 0.0, COT[rows, :].astype(F32))
+            grad = jnp.where(which % SEG == 0, GS[i // 2][0:1, :], COT[rows, :].astype(F32))
             scaled = SC2[rows, :]
             fed = normalize_back(grad, scaled, INV2[rows, 0:1], g01)
             GF[rows, :] = fed
@@ -602,14 +588,11 @@
         NV[1:2, :] = gains
         NV[3:4, :] = shifts
 
-    norm_two_back()
-    transpose_into(FDLT, FDL)
-
     def grad_unit(k, r):
         return W.at[UP, r] if k == ATT else G.at[k - 1, r]
 
-    order = [(DOWN, 1), (UP, 1), (DOWN, 2), (UP, 2), (DOWN, 3), (UP, 3), (DOWN, 0), (UP, 0)]
-    order += [(ATT, 1), (ATT, 2), (ATT, 3), (ATT, 0)]
+    turn = (2, 3, 1, 0)
+    order = [(k, r) for r in turn for k in (DOWN, UP)] + [(ATT, r) for r in turn]
     s0, sa1, sb1, sa2, sb2, sz = {}, {}, {}, {}, {}, {}
 
     def sum_start(i):
@@ -678,14 +661,12 @@
         for start, size, value in parts:
             ref[:, :, :, :, start : start + size] = value().astype(BF16).reshape(2, 2, 2, BLK, size)
 
-    def store_ffn(k, r, lhs_t, rhs, extra=None):
+    def store_ffn(k, r, lhs_t, rhs):
         ref = grad_unit(k, r)
 
         def block(n, carry):
             part = pl.ds(pl.multiple_of(n * 256, 256), 256)
             value = mm(lhs_t[...], rhs[:, part])
-            if extra is not None:
-                value = value + mm(extra[0][...], extra[1][:, part])
             ref[:, :, :, :, part] = value.astype(BF16).reshape(2, 2, 2, BLK, 256)
             return carry
 
@@ -703,15 +684,53 @@
 
     live = {}
 
+    def token_one():
+        unit = W.at[ATT, z]
+        kv_weight = jnp.concatenate([unit[0, 1].reshape(192, 768), unit[1, 0].reshape(192, 768)], axis=0)
+
+        def rows_of(i, carry):
+            rows = pl.ds(pl.multiple_of(i * 256, 256), 256)
+            ACT[i, :, 0:384] = mm_nt(XA[rows, :], kv_weight).astype(BF16)
+            return carry
+
+        lax.fori_loop(0, 4, rows_of, 0)
+        x8 = jnp.concatenate([XA[i * SEG : i * SEG + 16, :].astype(F32)[0:1] for i in range(8)], axis=0)
+        live["x8"] = x8
+        q8 = mm_nt(x8.astype(BF16), unit[0, 0].reshape(192, 768)).astype(BF16).astype(F32)
+        row = lax.broadcasted_iota(jnp.int32, (8, 1024), 0)
+        keep = lax.broadcasted_iota(jnp.int32, (8, 1024), 1) // SEG == row
+        mixes = []
+        for h in range(3):
+            q = q8[:, h * 64 : h * 64 + 64].astype(BF16)
+            parts = [mm_nt(q, ACT[i, :, h * 64 : h * 64 + 64]) for i in range(4)]
+            scores = jnp.where(keep, jnp.concatenate(parts, axis=1) * SCALE, -3.0e38)
+            top = jnp.max(scores, axis=-1, keepdims=True)
+            expd = jnp.exp(scores - top)
+            prob = (expd * (1.0 / jnp.sum(expd, axis=-1, keepdims=True))).astype(BF16)
+            mix = None
+            for i in range(4):
+                val = ACT[i, :, 192 + h * 64 : 256 + h * 64]
+                part = mm(prob[:, i * 256 : i * 256 + 256], val)
+                mix = part if mix is None else mix + part
+            mixes.append(mix)
+        exchange(0, mm(jnp.concatenate(mixes, axis=-1).astype(BF16), out_rows(unit)))
+
+    def token_two():
+        attended = exchange_sum(0)
+        scaled, _ = normalize(live["x8"] + attended)
+        first = scaled * g00 + b00
+        live["first8"] = first
+        loads["wu"].wait()
+        loads["wd"].wait()
+        active, _ = gelu_pair(mm(first.astype(BF16), cols(UP, 0, 0, 768)))
+        exchange(1, mm(active.astype(BF16), cols(DOWN, 0, 0, 768)))
+
     def cross_one():
-        exchange_wait(0)
-        live["sc2"] = assemble(0, 0)
-        first8 = assemble(0, 2)
-        live["inv2"] = assemble(0, 4)[:, 0:1]
-        summary = live["sc2"] * g01 + b01
+        fed = exchange_sum(1)
+        scaled, _ = normalize(live["first8"] + fed)
+        summary = scaled * g01 + b01
         live["summary"] = summary
         live["summary_low"] = summary.astype(BF16)
-        live["first8_low"] = first8.astype(BF16)
         for name in ("l1qk", "l1v", "l1o"):
             loads[name].wait()
         qkv = mm_nt(live["summary_low"], qkv_rows(L1.at[ATT])).astype(BF16).astype(F32)
@@ -733,10 +752,10 @@
             mixes.append(mm(prob.astype(BF16), val))
         mix = jnp.concatenate(mixes, axis=-1).astype(BF16)
         live["mix"] = mix
-        exchange(1, mm(mix, out_rows(L1.at[ATT])))
+        exchange(2, mm(mix, out_rows(L1.at[ATT])))
 
     def cross_two():
-        attended = exchange_sum(1)
+        attended = exchange_sum(2)
         live["xs1"], live["xi1"] = normalize(live["summary"] + attended)
         first = live["xs1"] * g10 + b10
         live["xfirst"] = first
@@ -745,14 +764,14 @@
         loads["l1d"].wait()
         active, live["xdg"] = gelu_pair(mm(live["xfirst_low"], l1(UP, 0, 768)))
         live["xact"] = active.astype(BF16)
-        exchange(2, mm(live["xact"], l1(DOWN, 0, 768)))
+        exchange(3, mm(live["xact"], l1(DOWN, 0, 768)))
 
     def cross_three():
-        fed = exchange_sum(2)
+        fed = exchange_sum(3)
         xs2, xi2 = normalize(live["xfirst"] + fed)
         upper = xs2 * g11 + b11
         for j in range(2):
-            out_ref[0, j * 128 : j * 128 + 1, :] = own_row(upper, j).astype(BF16)
+            GS[j, 1:2, :] = own_row(upper, j)
         loads["c8"].wait()
         grad_top = C8[...].astype(F32)[:, 0, :]
         live["xs2"], live["xi2"] = xs2, xi2
@@ -763,10 +782,10 @@
         live["xfed_low"] = grad_fed.astype(BF16)
         ga = mm_nt(live["xfed_low"], l1(DOWN, 0, 768))
         live["xgu"] = (ga * live["xdg"]).astype(BF16)
-        exchange(3, mm_nt(live["xgu"], l1(UP, 0, 768)))
+        exchange(4, mm_nt(live["xgu"], l1(UP, 0, 768)))
 
     def cross_four():
-        grad_first = live["xgf"] + exchange_sum(3)
+        grad_first = live["xgf"] + exchange_sum(4)
         grad_att = normalize_back(grad_first, live["xs1"], live["xi1"], g10)
         NV[4:5, :] = jnp.sum(grad_first * live["xs1"], axis=0, keepdims=True)
         NV[6:7, :] = jnp.sum(grad_first, axis=0, keepdims=True)
@@ -786,28 +805,16 @@
             gvs.append(mm_tn(prob.astype(BF16), gmh)[0:8, :])
         gqkv = jnp.concatenate(gqs + gks + gvs, axis=-1).astype(BF16)
         live["xgqkv"] = gqkv
-        exchange(4, mm(gqkv, qkv_rows(L1.at[ATT])))
+        exchange(5, mm(gqkv, qkv_rows(L1.at[ATT])))
 
     def cross_five():
-        grad_summary = live["xga"] + exchange_sum(4)
-        mine = jnp.where(pair_of == z, grad_summary, 0.0)
-        NV[1:2, :] += jnp.sum(mine * live["sc2"], axis=0, keepdims=True)
-        NV[3:4, :] += jnp.sum(mine, axis=0, keepdims=True)
-        gfed8 = normalize_back(grad_summary, live["sc2"], live["inv2"], g01)
-        live["gfed8"] = gfed8
-        fed8_low = gfed8.astype(BF16)
-        live["fed8_low"] = fed8_low
-        active, slope = gelu_pair(mm(live["first8_low"], cols(UP, 0, 0, 768)))
-        live["act8"] = active.astype(BF16)
-        ga = mm_nt(fed8_low, cols(DOWN, 0, 0, 768))
-        live["gu8"] = (ga * slope).astype(BF16)
-        exchange(5, mm_nt(live["gu8"], cols(UP, 0, 0, 768)))
-
-    def cross_six():
-        part = exchange_sum(5)
+        grad_summary = live["xga"] + exchange_sum(5)
         for j in range(2):
-            GF[j * 128 : j * 128 + 1, :] = own_row(live["gfed8"], j)
-            ACC[j * 128 : j * 128 + 1, :] = own_row(part, j)
+            GS[j, 0:1, :] = own_row(grad_summary, j)
+
+    def output_rows():
+        for j in range(2):
+            out_ref[0, j * 128 : j * 128 + 1, :] = GS[j, 1:2, :].astype(BF16)
 
     def norm_one_back():
         def chunk(i, rows, carry):
@@ -828,7 +835,7 @@
         NV[2:3, :] = shifts
 
     def attn_backward(r, first):
-        GM[...] = mm_nt(FDL[...], out_rows(W.at[ATT, r])).astype(BF16)
+        GM[...] = mm_nt(FDL[...], out_rows(W.at[ATT, z_of[r]])).astype(BF16)
 
         def segment(s, carry):
             rows = pl.ds(pl.multiple_of(s * SEG, SEG), SEG)
@@ -858,7 +865,7 @@
                 (576, 192, lambda: mm(FDLT[...], MIX[r])),
             ],
         )
-        accumulate(first, mm(GQ[...], qkv_rows(W.at[ATT, r])))
+        accumulate(first, mm(GQ[...], qkv_rows(W.at[ATT, z_of[r]])))
 
     fac = {}
 
@@ -942,52 +949,66 @@
         crossg_ref[0] = total[4:6, 0:BLK]
         crossg_ref[1] = total[6:8, 0:BLK]
 
-    def eight_turned(dst, value):
-        full = jnp.concatenate([value.astype(F32), jnp.zeros((120, 768), F32)], axis=0)
-        dst[...] = full.T.astype(BF16)
-
-    def eight_rows(dst, value):
-        dst[...] = jnp.concatenate([value.astype(F32), jnp.zeros((120, 768), F32)], axis=0).astype(BF16)
-
+    for name in ("wqk", "wv", "wo"):
+        loads[name].wait()
+    z_own(ATT)
+    loads["x"].wait()
+    token_one()
+    gather_tick(0)
+    z_own(UP)
+    attn_forward(0)
+    gather_tick(1)
+    token_two()
+    gather_tick(2)
+    z_own(DOWN)
     cross_one()
-    ffn_back_one(1)
-    store_ffn(DOWN, 1, FDLT, ACT.at[1])
-    sum_start(0)
-    store_ffn(UP, 1, FLT, GU)
-    sum_start(1)
-    ffn_back_two(1, True)
+    gather_tick(3)
+    attn_forward(1)
+    transpose_into(XT, XA, z * 256)
+    gather_tick(4)
     cross_two()
-    pump(0)
-    ffn_back_one(2)
-    store_ffn(DOWN, 2, FDLT, ACT.at[2])
-    sum_start(2)
-    store_ffn(UP, 2, FLT, GU)
-    sum_start(3)
-    ffn_back_two(2, False)
+    attn_forward(2)
+    gather_tick(5)
     cross_three()
-    pump(1)
-    ffn_back_one(3)
-    store_ffn(DOWN, 3, FDLT, ACT.at[3])
-    sum_start(4)
-    store_ffn(UP, 3, FLT, GU)
-    sum_start(5)
-    ffn_back_two(3, False)
+    attn_forward(3)
+    norm_one()
+    gather_tick(6)
     cross_four()
+    ffn_forward(0)
+    ffn_forward(1)
+    gather_tick(7)
+    cross_five()
+    ffn_forward(2)
+    gather_tick(8)
+    ffn_forward(3)
+    ffn_down(0)
+    gather_tick(9)
+    ffn_down(1)
+    transpose_into(FLT, FL)
+    gather_tick(10)
     factor_start()
-    pump(2)
-    cross_five()
-    pump(3)
-    ffn_back_one(0)
-    eight_turned(EL, live["fed8_low"])
-    eight_rows(ER, live["act8"])
-    store_ffn(DOWN, 0, FDLT, ACT.at[0], (EL, ER))
-    sum_start(6)
-    eight_turned(EL, live["first8_low"])
-    eight_rows(ER, live["gu8"])
-    store_ffn(UP, 0, FLT, GU, (EL, ER))
-    sum_start(7)
-    ffn_back_two(0, False)
-    cross_six()
+    ffn_down(2)
+    gather_tick(11)
+    ffn_down(3)
+    norm_two()
+    output_rows()
+    factor_two()
+    loads["cot"].wait()
+    norm_two_back()
+    transpose_into(FDLT, FDL)
+
+    step = 0
+    for n, r in enumerate(turn):
+        ffn_back_one(r)
+        store_ffn(DOWN, r, FDLT, ACT.at[r])
+        sum_start(2 * n)
+        store_ffn(UP, r, FLT, GU)
+        sum_start(2 * n + 1)
+        ffn_back_two(r, n == 0)
+        if n == 0:
+            factor_three()
+        pump(step)
+        step += 1
     norm_one_back()
     norm_grads_start()
     transpose_into(FDLT, FDL)
@@ -995,30 +1016,29 @@
         for i in range(9):
             table[i].wait_send()
             waited.append(id(table[i]))
-    pump(4)
-    factor_two()
-    attn_backward(1, True)
-    sum_start(8)
-    pump(5)
-    factor_three()
-    norm_grads_two()
-    attn_backward(2, False)
-    sum_start(9)
-    pump(6)
-    attn_backward(3, False)
-    sum_start(10)
-    pump(7)
-    attn_backward(0, False)
-    sum_start(11)
+    for condition, copy in passed:
+
+        @pl.when(condition)
+        def _(copy=copy):
+            copy.wait_send()
+
+    pump(step)
+    step += 1
+    factor_final()
+    for n, r in enumerate(turn):
+        attn_backward(r, n == 0)
+        sum_start(8 + n)
+        pump(step)
+        step += 1
+        if n == 1:
+            norm_grads_two()
     ing_ref[0] = (GF[...] + ACC[...]).astype(BF16)
-    pump(8)
-    factor_final()
+    norm_grads_final()
     pump(9)
-    norm_grads_final()
+    write_unit(0, DOWN, sum_final(DOWN))
     pump(10)
-    write_unit(0, DOWN, sum_final(DOWN))
+    write_unit(0, UP, sum_final(UP))
     pump(11)
-    write_unit(0, UP, sum_final(UP))
     pump(12)
     pump(13)
     write_unit(0, ATT, sum_final(ATT))
@@ -1076,7 +1096,7 @@
             pltpu.VMEM((12, HALF, 768), BF16),
             pltpu.VMEM((3, 3, BLK, 768), BF16),
             pltpu.VMEM((3,) + blocks, BF16),
-            pltpu.VMEM((256, 768), BF16),
+            pltpu.VMEM((1024, 768), BF16),
             pltpu.VMEM((256, 768), BF16),
             pltpu.VMEM((4, 256, 576), BF16),
             pltpu.VMEM((4, 3, 256, 128), F32),
@@ -1100,15 +1120,16 @@
             pltpu.VMEM((256, 128), F32),
             pltpu.VMEM((2, 2, 2, 64, 768), BF16),
             pltpu.VMEM((768, 256), BF16),
-            pltpu.VMEM((768, 128), BF16),
-            pltpu.VMEM((128, 768), BF16),
+            pltpu.VMEM((2, 8, 768), F32),
             pltpu.VMEM((7, 4, 8, 768), F32),
             pltpu.VMEM((8, 768), F32),
             pltpu.VMEM((2, 2, 2, 8, 128), F32),
             pltpu.VMEM((7, 8, 128), F32),
             sem((13,)),
-            sem((6, 9)),
-            sem((6, 9)),
+            sem((12, 2)),
+            sem((12,)),
+            sem((5, 9)),
+            sem((5, 9)),
             sem((6, 12)),
             sem((6, 12)),
             sem((7, 3)),

time: 154 us -> 147 us (0.955)
  Pallas kernels: 152 us -> 146 us
    pallas_call x1, Pallas kernels: 150 us -> 143 us  [fused_body(): pl.pallas_call(fused_kernel, out_shape=(jax.ShapeDtypeStruct((1, 256, 768...]
where the time goes in v3:
time: 147 us; the launch traced here: 146 us
  Pallas kernels  146 us (99%)
    pallas_call x1, Pallas kernels, fused_body(): pl.pallas_call(fused_kernel, out_shape=(jax.ShapeDtypeStruct((1, 256, 768...  143 us

profile of v3, /device:TPU:0, one launch (start us, length us, event | category | flops | bytes accessed | tf_op | source)
XLA Modules:
  0.0 146.4 jit_solution(13299436216144831769)
XLA Ops:
  0.6 142.8 %shard_map.160 = (bf16[1,256,768]{2,1,0:T(8,128)(2,1)}, bf16[1,256,768]{2,1,0:T(8,128)(2,1)}, f32[2,3,96,192]{3,2,1,0:T(8,128)}, f32[2,192,96]{2,1,0:T(8,128)}, ...) custom-call(bf16[1,1024,768]{2,1,0:T(8,128)(2,1)} %tokens_hbm.1, ...), custom_call_target="tpu_custom_call" | custom-call | tf_op jit(solution)/shard_map/pallas_call | solution.py:1074
  143.5 2.7 %shard_map.161 = (bf16[1,256,768]{2,1,0:T(8,128)(2,1)}, bf16[1,256,768]{2,1,0:T(8,128)(2,1)}, f32[2,3,96,192]{3,2,1,0:T(8,128)}, f32[2,192,96]{2,1,0:T(8,128)}, ...) custom-call(bf16[1,256,768]{2,1,0:T(8,128)(2,1)} %get-tuple-element., ...), custom_call_target="tpu_custom_call" | custom-call | tf_op jit(solution)/shard_map/pallas_call | solution.py:1148

commit v4 on v3

--- a/solution.py
+++ b/solution.py
@@ -321,7 +321,7 @@
 def fused_kernel(
     tokens_hbm, cot_hbm, cot_seg, doc_ref, wq_hbm, wo_hbm, wu_hbm, wd_hbm, gain_ref, shift_ref,
     out_ref, ing_ref, qkvg_ref, outg_ref, upg_ref, downg_ref, gaing_ref, shiftg_ref, crossg_ref,
-    W, G, RC, RA1, RB1, RA2, RB2, RZ, L1, XA, COT, QKV, PR, MIX, ACT, DG, GU, GQ, ACC, SC1, SC2, GF,
+    W, G, RC, RA1, RB1, RA2, RB2, RZ, RZF, RF, L1, XA, COT, QKV, PR, MIX, ACT, DG, GU, GQ, ACC, SC1, SC2, GF,
     FL, FLT, FDL, FDLT, XT, GM, C8, INV1, INV2, FAC, LT, GS, E, NV, SV, RSV,
     sem_local, zg_s, zg_r, ag_s, ag_r, rs_s, rs_r, e_s, e_r, f_s, f_r, v_s, v_r,
 ):
@@ -384,7 +384,7 @@
     pl.semaphore_wait(barrier, 10)
 
     own_unit = [W.at[ATT, z], wu_hbm.at[0], wd_hbm.at[0]]
-    units = [(k, r) for k in (ATT, UP, DOWN) for r in (1, 2, 3)]
+    units = [(ATT, 1), (UP, 1), (ATT, 2), (ATT, 3), (UP, 2), (DOWN, 1), (UP, 3), (DOWN, 2), (DOWN, 3)]
     a1, b1, a2, b2, cc = {}, {}, {}, {}, {}
     passed = []
 
@@ -424,34 +424,33 @@
 
             pass_on(further, copy)
 
-    def gather_tick(t):
-        i = t
-        if 0 <= i < 9:
-            k, r = units[i]
-            z_step(k, r - 1)
-            part = W.at[k, z_of[r], y, x, c, pl.ds(0, HALF)]
-            a1[i] = remote(part, part, ag_s.at[0, i], ag_r.at[0, i], x_peer)
-            part = W.at[k, z_of[r], y, x, c, pl.ds(HALF, HALF)]
-            b1[i] = remote(part, part, ag_s.at[1, i], ag_r.at[1, i], y_peer)
-        i = t - 1
-        if 0 <= i < 9:
-            k, r = units[i]
-            a1[i].wait_recv()
-            part = W.at[k, z_of[r], y, :, c, pl.ds(0, HALF)]
-            a2[i] = remote(part, part, ag_s.at[2, i], ag_r.at[2, i], y_peer)
-            b1[i].wait_recv()
-            part = W.at[k, z_of[r], :, x, c, pl.ds(HALF, HALF)]
-            b2[i] = remote(part, part, ag_s.at[3, i], ag_r.at[3, i], x_peer)
-        i = t - 2
-        if 0 <= i < 9:
-            k, r = units[i]
-            a2[i].wait_recv()
-            b2[i].wait_recv()
-            part = W.at[k, z_of[r], :, :, c]
-            cc[i] = remote(part, part, ag_s.at[4, i], ag_r.at[4, i], core_peer)
-        i = t - 3
-        if 0 <= i < 9:
-            cc[i].wait_recv()
+    def gather_a(i):
+        k, r = units[i]
+        z_step(k, r - 1)
+        part = W.at[k, z_of[r], y, x, c, pl.ds(0, HALF)]
+        a1[i] = remote(part, part, ag_s.at[0, i], ag_r.at[0, i], x_peer)
+        part = W.at[k, z_of[r], y, x, c, pl.ds(HALF, HALF)]
+        b1[i] = remote(part, part, ag_s.at[1, i], ag_r.at[1, i], y_peer)
+
+    def gather_b(i):
+        k, r = units[i]
+        a1[i].wait_recv()
+        part = W.at[k, z_of[r], y, :, c, pl.ds(0, HALF)]
+        a2[i] = remote(part, part, ag_s.at[2, i], ag_r.at[2, i], y_peer)
+        b1[i].wait_recv()
+        part = W.at[k, z_of[r], :, x, c, pl.ds(HALF, HALF)]
+        b2[i] = remote(part, part, ag_s.at[3, i], ag_r.at[3, i], x_peer)
+
+    def gather_c(i):
+        k, r = units[i]
+        a2[i].wait_recv()
+        b2[i].wait_recv()
+        part = W.at[k, z_of[r], :, :, c]
+        cc[i] = remote(part, part, ag_s.at[4, i], ag_r.at[4, i], core_peer)
+
+    def arrived(k, r):
+        if r:
+            cc[units.index((k, r))].wait_recv()
 
     def unit_value(ref):
         return ref[...].reshape(768, ref.shape[-1])
@@ -472,6 +471,7 @@
             ACC[...] += value
 
     def attn_forward(r):
+        arrived(ATT, r)
         QKV[r] = mm_nt(XA[own_rows, :], qkv_rows(W.at[ATT, z_of[r]])).astype(BF16)
 
         def segment(s, carry):
@@ -519,6 +519,7 @@
         row_chunks(chunk)
 
     def ffn_forward(r):
+        arrived(UP, r)
         def block(n, carry):
             part = pl.ds(pl.multiple_of(n * 256, 256), 256)
             upward = mm(FL[...], unit_value(W.at[UP, z_of[r], :, :, :, :, part]))
@@ -530,6 +531,7 @@
         lax.fori_loop(0, 3, block, 0)
 
     def ffn_down(r):
+        arrived(DOWN, r)
         accumulate(r == 0, mm(ACT[r], cols(DOWN, r, 0, 768)))
 
     def norm_two():
@@ -591,9 +593,9 @@
     def grad_unit(k, r):
         return W.at[UP, r] if k == ATT else G.at[k - 1, r]
 
-    turn = (2, 3, 1, 0)
+    turn = (3, 2, 1, 0)
     order = [(k, r) for r in turn for k in (DOWN, UP)] + [(ATT, r) for r in turn]
-    s0, sa1, sb1, sa2, sb2, sz = {}, {}, {}, {}, {}, {}
+    s0, sa1, sb1, sa2, sb2, sza, szb, sfa, sfb = {}, {}, {}, {}, {}, {}, {}, {}, {}
 
     def sum_start(i):
         k, r = order[i]
@@ -603,9 +605,9 @@
     def add_low(a, b):
         return (a.astype(F32) + b.astype(F32)).astype(BF16)
 
+    top, low = pl.ds(0, HALF), pl.ds(HALF, HALF)
+
     def sum_one(i):
-        if not 0 <= i < 12:
-            return
         k, r = order[i]
         g = grad_unit(k, r)
         s0[i].wait_recv()
@@ -616,46 +618,89 @@
             return carry
 
         lax.fori_loop(0, 4, block, 0)
-        sa1[i] = remote(g.at[:, nx, c, pl.ds(0, HALF)], RA1.at[i], rs_s.at[1, i], rs_r.at[1, i], x_peer)
-        sb1[i] = remote(g.at[ny, :, c, pl.ds(HALF, HALF)], RB1.at[i], rs_s.at[2, i], rs_r.at[2, i], y_peer)
+        if k == ATT:
+            part_a, part_b = g.at[:, nx, c, top], g.at[ny, :, c, low]
+            peer_a, peer_b = x_peer, y_peer
+        else:
+            part_a, part_b = g.at[ny, :, c, top], g.at[:, nx, c, low]
+            peer_a, peer_b = y_peer, x_peer
+        sa1[i] = remote(part_a, RA1.at[i], rs_s.at[1, i], rs_r.at[1, i], peer_a)
+        sb1[i] = remote(part_b, RB1.at[i], rs_s.at[2, i], rs_r.at[2, i], peer_b)
 
     def sum_two(i):
-        if not 0 <= i < 12:
-            return
         k, r = order[i]
         g = grad_unit(k, r)
         sa1[i].wait_recv()
-        for j in range(2):
-            g[j, x, c, 0:HALF, :] = add_low(g[j, x, c, 0:HALF, :], RA1[i, j])
-        sa2[i] = remote(g.at[ny, x, c, pl.ds(0, HALF)], RA2.at[i], rs_s.at[3, i], rs_r.at[3, i], y_peer)
-        sb1[i].wait_recv()
-        for j in range(2):
-            g[y, j, c, HALF:BLK, :] = add_low(g[y, j, c, HALF:BLK, :], RB1[i, j])
-        sb2[i] = remote(g.at[y, nx, c, pl.ds(HALF, HALF)], RB2.at[i], rs_s.at[4, i], rs_r.at[4, i], x_peer)
+        if k == ATT:
+            for j in range(2):
+                g[j, x, c, 0:HALF, :] = add_low(g[j, x, c, 0:HALF, :], RA1[i, j])
+            sa2[i] = remote(g.at[ny, x, c, top], RA2.at[i - 8], rs_s.at[3, i], rs_r.at[3, i], y_peer)
+            sb1[i].wait_recv()
+            for j in range(2):
+                g[y, j, c, HALF:BLK, :] = add_low(g[y, j, c, HALF:BLK, :], RB1[i, j])
+            sb2[i] = remote(g.at[y, nx, c, low], RB2.at[i - 8], rs_s.at[4, i], rs_r.at[4, i], x_peer)
+        else:
+            sb1[i].wait_recv()
+            for j in range(2):
+                g[y, j, c, 0:HALF, :] = add_low(g[y, j, c, 0:HALF, :], RA1[i, j])
+                g[j, x, c, HALF:BLK, :] = add_low(g[j, x, c, HALF:BLK, :], RB1[i, j])
 
     def sum_three(i):
-        if not 0 <= i < 12:
-            return
+        g = grad_unit(*order[i])
+        sa2[i].wait_recv()
+        g[y, x, c, 0:HALF, :] = add_low(g[y, x, c, 0:HALF, :], RA2[i - 8])
+        sb2[i].wait_recv()
+        g[y, x, c, HALF:BLK, :] = add_low(g[y, x, c, HALF:BLK, :], RB2[i - 8])
+
+    landing = {1: 0, 3: 1, 2: 2}
+
+    def z_wait(k, r):
+        i = order.index((k, r))
+        sza[i].wait_recv()
+        if k != ATT:
+            szb[i].wait_recv()
+
+    def z_add(k, g, slot):
+        if k == ATT:
+            g[y, x, c] = add_low(g[y, x, c], RZ[slot])
+        else:
+            for j in range(2):
+                g[y, j, c, 0:HALF, :] = add_low(g[y, j, c, 0:HALF, :], RZF[k - 1, slot, 0, j])
+                g[j, x, c, HALF:BLK, :] = add_low(g[j, x, c, HALF:BLK, :], RZF[k - 1, slot, 1, j])
+
+    def sum_z(i):
         k, r = order[i]
         g = grad_unit(k, r)
-        sa2[i].wait_recv()
-        g[y, x, c, 0:HALF, :] = add_low(g[y, x, c, 0:HALF, :], RA2[i])
-        sb2[i].wait_recv()
-        g[y, x, c, HALF:BLK, :] = add_low(g[y, x, c, HALF:BLK, :], RB2[i])
+        if r == 2:
+            z_wait(k, 3)
+            z_add(k, g, landing[3])
         if r:
-            sz[k, r] = remote(g.at[y, x, c], RZ.at[k, r - 1], rs_s.at[5, i], rs_r.at[5, i], z_peer[r])
-
-    def pump(i):
-        sum_one(i)
-        sum_two(i - 1)
-        sum_three(i - 2)
+            peer = z_peer[2] if r == 2 else z_peer[1]
+            if k == ATT:
+                sza[i] = remote(g.at[y, x, c], RZ.at[landing[r]], rs_s.at[5, i], rs_r.at[5, i], peer)
+            else:
+                land = RZF.at[k - 1, landing[r]]
+                sza[i] = remote(g.at[y, :, c, top], land.at[0], rs_s.at[5, i], rs_r.at[5, i], peer)
+                szb[i] = remote(g.at[:, x, c, low], land.at[1], rs_s.at[6, i], rs_r.at[6, i], peer)
+        else:
+            z_wait(k, 1)
+            z_wait(k, 2)
+            if k != ATT:
+                for j in range(2):
+                    a, b = RZF[k - 1, 0, 0, j].astype(F32), RZF[k - 1, 2, 0, j].astype(F32)
+                    g[y, j, c, 0:HALF, :] = add_low(g[y, j, c, 0:HALF, :], a + b)
+                    a, b = RZF[k - 1, 0, 1, j].astype(F32), RZF[k - 1, 2, 1, j].astype(F32)
+                    g[j, x, c, HALF:BLK, :] = add_low(g[j, x, c, HALF:BLK, :], a + b)
+                sfa[k] = remote(g.at[y, nx, c, top], RF.at[k - 1, 0], rs_s.at[7, k], rs_r.at[7, k], x_peer)
+                sfb[k] = remote(g.at[ny, x, c, low], RF.at[k - 1, 1], rs_s.at[8, k], rs_r.at[8, k], y_peer)
 
     def sum_final(k):
-        for r in range(1, 4):
-            sz[k, r].wait_recv()
-        g = grad_unit(k, 0)
-        own = g[y, x, c].astype(F32) + RZ[k, 0].astype(F32)
-        return own + (RZ[k, 1].astype(F32) + RZ[k, 2].astype(F32))
+        own = grad_unit(k, 0)[y, x, c].astype(F32)
+        if k == ATT:
+            return own + (RZ[0].astype(F32) + RZ[2].astype(F32))
+        sfa[k].wait_recv()
+        sfb[k].wait_recv()
+        return own + jnp.concatenate([RF[k - 1, 0], RF[k - 1, 1]], axis=0).astype(F32)
 
     def store_unit(ref, parts):
         for start, size, value in parts:
@@ -676,8 +721,16 @@
         ga = mm_nt(FDL[...], cols(DOWN, r, 0, 768))
         GU[...] = (ga * DG[r].astype(F32)).astype(BF16)
 
-    def ffn_back_two(r, first):
-        accumulate(first, mm_nt(GU[...], cols(UP, r, 0, 768)))
+    def ffn_back_two(r):
+        accumulate(r == turn[0], mm_nt(GU[...], cols(UP, r, 0, 768)))
+
+    def grad_down(r):
+        store_ffn(DOWN, r, FDLT, ACT.at[r])
+        sum_start(order.index((DOWN, r)))
+
+    def grad_up(r):
+        store_ffn(UP, r, FLT, GU)
+        sum_start(order.index((UP, r)))
 
     def l1(k, start, size):
         return unit_value(L1.at[k, :, :, :, :, pl.ds(start, size)])
@@ -834,7 +887,7 @@
         NV[0:1, :] = gains
         NV[2:3, :] = shifts
 
-    def attn_backward(r, first):
+    def attn_backward(r):
         GM[...] = mm_nt(FDL[...], out_rows(W.at[ATT, z_of[r]])).astype(BF16)
 
         def segment(s, carry):
@@ -865,7 +918,8 @@
                 (576, 192, lambda: mm(FDLT[...], MIX[r])),
             ],
         )
-        accumulate(first, mm(GQ[...], qkv_rows(W.at[ATT, z_of[r]])))
+        sum_start(order.index((ATT, r)))
+        accumulate(r == turn[0], mm(GQ[...], qkv_rows(W.at[ATT, z_of[r]])))
 
     fac = {}
 
@@ -949,98 +1003,150 @@
         crossg_ref[0] = total[4:6, 0:BLK]
         crossg_ref[1] = total[6:8, 0:BLK]
 
+    def turn_to_attention():
+        norm_one_back()
+        norm_grads_start()
+        transpose_into(FDLT, FDL)
+        for table in (a1, b1, a2, b2, cc):
+            for i in range(9):
+                table[i].wait_send()
+                waited.append(id(table[i]))
+        for condition, copy in passed:
+
+            @pl.when(condition)
+            def _(copy=copy):
+                copy.wait_send()
+
     for name in ("wqk", "wv", "wo"):
         loads[name].wait()
     z_own(ATT)
+    z_own(UP)
     loads["x"].wait()
     token_one()
-    gather_tick(0)
-    z_own(UP)
     attn_forward(0)
-    gather_tick(1)
+    gather_a(0)
+    transpose_into(XT, XA, z * 256)
+    gather_a(1)
+    gather_b(0)
     token_two()
-    gather_tick(2)
+    gather_a(2)
+    gather_b(1)
     z_own(DOWN)
+    gather_c(0)
     cross_one()
-    gather_tick(3)
+    gather_b(2)
     attn_forward(1)
-    transpose_into(XT, XA, z * 256)
-    gather_tick(4)
+    gather_c(1)
+    gather_a(3)
+    gather_a(4)
+    gather_a(5)
     cross_two()
+    gather_c(2)
+    gather_b(3)
     attn_forward(2)
-    gather_tick(5)
+    gather_b(4)
+    gather_b(5)
+    gather_a(6)
+    gather_a(7)
     cross_three()
+    gather_c(3)
     attn_forward(3)
+    gather_c(4)
+    gather_a(8)
+    cross_four()
+    gather_c(5)
     norm_one()
-    gather_tick(6)
-    cross_four()
     ffn_forward(0)
+    gather_b(6)
+    ffn_down(0)
+    gather_b(7)
+    cross_five()
     ffn_forward(1)
-    gather_tick(7)
-    cross_five()
+    gather_b(8)
+    factor_start()
+    ffn_down(1)
     ffn_forward(2)
-    gather_tick(8)
+    transpose_into(FLT, FL)
+    gather_c(6)
     ffn_forward(3)
-    ffn_down(0)
-    gather_tick(9)
-    ffn_down(1)
-    transpose_into(FLT, FL)
-    gather_tick(10)
-    factor_start()
+    gather_c(7)
     ffn_down(2)
-    gather_tick(11)
+    gather_c(8)
     ffn_down(3)
+    factor_two()
     norm_two()
     output_rows()
-    factor_two()
     loads["cot"].wait()
     norm_two_back()
     transpose_into(FDLT, FDL)
-
-    step = 0
-    for n, r in enumerate(turn):
-        ffn_back_one(r)
-        store_ffn(DOWN, r, FDLT, ACT.at[r])
-        sum_start(2 * n)
-        store_ffn(UP, r, FLT, GU)
-        sum_start(2 * n + 1)
-        ffn_back_two(r, n == 0)
-        if n == 0:
-            factor_three()
-        pump(step)
-        step += 1
-    norm_one_back()
-    norm_grads_start()
-    transpose_into(FDLT, FDL)
-    for table in (a1, b1, a2, b2, cc):
-        for i in range(9):
-            table[i].wait_send()
-            waited.append(id(table[i]))
-    for condition, copy in passed:
-
-        @pl.when(condition)
-        def _(copy=copy):
-            copy.wait_send()
-
-    pump(step)
-    step += 1
+    ffn_back_one(3)
+    grad_down(3)
+    grad_up(3)
+    ffn_back_two(3)
+    ffn_back_one(2)
+    sum_one(0)
+    grad_down(2)
+    sum_one(1)
+    grad_up(2)
+    ffn_back_two(2)
+    ffn_back_one(1)
+    sum_one(2)
+    grad_down(1)
+    sum_one(3)
+    grad_up(1)
+    sum_two(0)
+    sum_z(0)
+    ffn_back_two(1)
+    sum_one(4)
+    ffn_back_one(0)
+    sum_one(5)
+    grad_down(0)
+    grad_up(0)
+    sum_two(1)
+    sum_z(1)
+    ffn_back_two(0)
+    turn_to_attention()
+    sum_one(6)
+    sum_one(7)
+    sum_two(2)
+    attn_backward(3)
+    sum_two(3)
+    sum_z(2)
+    attn_backward(2)
+    sum_two(4)
+    sum_z(4)
+    sum_one(8)
+    attn_backward(1)
+    sum_two(5)
+    sum_z(3)
+    sum_z(5)
+    attn_backward(0)
+    sum_two(6)
+    factor_three()
+    ing_ref[0] = (GF[...] + ACC[...]).astype(BF16)
+    norm_grads_two()
+    sum_two(7)
+    sum_one(9)
     factor_final()
-    for n, r in enumerate(turn):
-        attn_backward(r, n == 0)
-        sum_start(8 + n)
-        pump(step)
-        step += 1
-        if n == 1:
-            norm_grads_two()
-    ing_ref[0] = (GF[...] + ACC[...]).astype(BF16)
+    sum_two(8)
+    sum_z(6)
+    sum_one(10)
+    sum_two(9)
+    sum_one(11)
+    sum_three(8)
+    sum_z(8)
+    write_unit(0, DOWN, sum_final(DOWN))
+    sum_two(10)
+    sum_three(9)
+    sum_z(9)
+    sum_z(7)
+    sum_two(11)
+    sum_three(10)
+    sum_z(10)
+    write_unit(0, UP, sum_final(UP))
+    sum_three(11)
+    sum_z(11)
     norm_grads_final()
-    pump(9)
-    write_unit(0, DOWN, sum_final(DOWN))
-    pump(10)
-    write_unit(0, UP, sum_final(UP))
-    pump(11)
-    pump(12)
-    pump(13)
     write_unit(0, ATT, sum_final(ATT))
     for copy in sends:
         if id(copy) not in waited:
@@ -1092,9 +1198,11 @@
             pltpu.VMEM((12, 2, 2, BLK, 768), BF16),
             pltpu.VMEM((12, 2, HALF, 768), BF16),
             pltpu.VMEM((12, 2, HALF, 768), BF16),
-            pltpu.VMEM((12, HALF, 768), BF16),
-            pltpu.VMEM((12, HALF, 768), BF16),
-            pltpu.VMEM((3, 3, BLK, 768), BF16),
+            pltpu.VMEM((4, HALF, 768), BF16),
+            pltpu.VMEM((4, HALF, 768), BF16),
+            pltpu.VMEM((3, BLK, 768), BF16),
+            pltpu.VMEM((2, 3, 2, 2, HALF, 768), BF16),
+            pltpu.VMEM((2, 2, HALF, 768), BF16),
             pltpu.VMEM((3,) + blocks, BF16),
             pltpu.VMEM((1024, 768), BF16),
             pltpu.VMEM((256, 768), BF16),
@@ -1130,8 +1238,8 @@
             sem((12,)),
             sem((5, 9)),
             sem((5, 9)),
-            sem((6, 12)),
-            sem((6, 12)),
+            sem((9, 12)),
+            sem((9, 12)),
             sem((7, 3)),
             sem((7, 3)),
             sem((3,)),

time: 147 us -> 135 us (0.918)
  Pallas kernels: 146 us -> 134 us
    pallas_call x1, Pallas kernels: 143 us -> 131 us  [fused_body(): pl.pallas_call(fused_kernel, out_shape=(jax.ShapeDtypeStruct((1, 256, 768...]
where the time goes in v4:
time: 135 us
  Pallas kernels  134 us (99%)
    pallas_call x1, Pallas kernels, fused_body(): pl.pallas_call(fused_kernel, out_shape=(jax.ShapeDtypeStruct((1, 256, 768...  131 us
    pallas_call x1, Pallas kernels, fused_body(): pl.pallas_call(settle_kernel, out_shape=tuple((jax.ShapeDtypeStruct(v.sha...  2.74 us

profile of v4, /device:TPU:0, one launch (start us, length us, event | category | flops | bytes accessed | tf_op | source)
XLA Modules:
  0.0 134.9 jit_solution(5731637578171840001)
XLA Ops:
  0.6 131.3 %shard_map.160 = (bf16[1,256,768]{2,1,0:T(8,128)(2,1)}, bf16[1,256,768]{2,1,0:T(8,128)(2,1)}, f32[2,3,96,192]{3,2,1,0:T(8,128)}, f32[2,192,96]{2,1,0:T(8,128)}, ...) custom-call(bf16[1,1024,768]{2,1,0:T(8,128)(2,1)} %tokens_hbm.1, ...), custom_call_target="tpu_custom_call" | custom-call | tf_op jit(solution)/shard_map/pallas_call | solution.py:1180
  132.0 2.7 %shard_map.161 = (bf16[1,256,768]{2,1,0:T(8,128)(2,1)}, bf16[1,256,768]{2,1,0:T(8,128)(2,1)}, f32[2,3,96,192]{3,2,1,0:T(8,128)}, f32[2,192,96]{2,1,0:T(8,128)}, ...) custom-call(bf16[1,256,768]{2,1,0:T(8,128)(2,1)} %get-tuple-element., ...), custom_call_target="tpu_custom_call" | custom-call | tf_op jit(solution)/shard_map/pallas_call | solution.py:1256

commit v5 on v4

--- a/solution.py
+++ b/solution.py
@@ -384,8 +384,8 @@
     pl.semaphore_wait(barrier, 10)
 
     own_unit = [W.at[ATT, z], wu_hbm.at[0], wd_hbm.at[0]]
-    units = [(ATT, 1), (UP, 1), (ATT, 2), (ATT, 3), (UP, 2), (DOWN, 1), (UP, 3), (DOWN, 2), (DOWN, 3)]
-    a1, b1, a2, b2, cc = {}, {}, {}, {}, {}
+    units = [(ATT, 1), (UP, 1), (ATT, 2), (ATT, 3), (DOWN, 1), (UP, 2), (UP, 3), (DOWN, 2), (DOWN, 3)]
+    a1, b1, a2, b2, a3, b3, cc = {}, {}, {}, {}, {}, {}, {}
     passed = []
 
     def z_copy(src, k, shard, side):
@@ -427,26 +427,28 @@
     def gather_a(i):
         k, r = units[i]
         z_step(k, r - 1)
-        part = W.at[k, z_of[r], y, x, c, pl.ds(0, HALF)]
-        a1[i] = remote(part, part, ag_s.at[0, i], ag_r.at[0, i], x_peer)
-        part = W.at[k, z_of[r], y, x, c, pl.ds(HALF, HALF)]
-        b1[i] = remote(part, part, ag_s.at[1, i], ag_r.at[1, i], y_peer)
+        upper = W.at[k, z_of[r], y, x, c, pl.ds(0, HALF)]
+        lower = W.at[k, z_of[r], y, x, c, pl.ds(HALF, HALF)]
+        a1[i] = remote(upper, upper, ag_s.at[0, i], ag_r.at[0, i], x_peer)
+        b1[i] = remote(lower, lower, ag_s.at[1, i], ag_r.at[1, i], y_peer)
+        a2[i] = remote(upper, upper, ag_s.at[2, i], ag_r.at[2, i], y_peer)
+        b2[i] = remote(lower, lower, ag_s.at[3, i], ag_r.at[3, i], x_peer)
 
     def gather_b(i):
         k, r = units[i]
         a1[i].wait_recv()
-        part = W.at[k, z_of[r], y, :, c, pl.ds(0, HALF)]
-        a2[i] = remote(part, part, ag_s.at[2, i], ag_r.at[2, i], y_peer)
+        part = W.at[k, z_of[r], y, nx, c, pl.ds(0, HALF)]
+        a3[i] = remote(part, part, ag_s.at[4, i], ag_r.at[4, i], y_peer)
         b1[i].wait_recv()
-        part = W.at[k, z_of[r], :, x, c, pl.ds(HALF, HALF)]
-        b2[i] = remote(part, part, ag_s.at[3, i], ag_r.at[3, i], x_peer)
+        part = W.at[k, z_of[r], ny, x, c, pl.ds(HALF, HALF)]
+        b3[i] = remote(part, part, ag_s.at[5, i], ag_r.at[5, i], x_peer)
 
     def gather_c(i):
         k, r = units[i]
-        a2[i].wait_recv()
-        b2[i].wait_recv()
+        for table in (a2, b2, a3, b3):
+            table[i].wait_recv()
         part = W.at[k, z_of[r], :, :, c]
-        cc[i] = remote(part, part, ag_s.at[4, i], ag_r.at[4, i], core_peer)
+        cc[i] = remote(part, part, ag_s.at[6, i], ag_r.at[6, i], core_peer)
 
     def arrived(k, r):
         if r:
@@ -1007,7 +1009,7 @@
         norm_one_back()
         norm_grads_start()
         transpose_into(FDLT, FDL)
-        for table in (a1, b1, a2, b2, cc):
+        for table in (a1, b1, a2, b2, a3, b3, cc):
             for i in range(9):
                 table[i].wait_send()
                 waited.append(id(table[i]))
@@ -1020,65 +1022,65 @@
     for name in ("wqk", "wv", "wo"):
         loads[name].wait()
     z_own(ATT)
-    z_own(UP)
     loads["x"].wait()
     token_one()
+    z_own(UP)
     attn_forward(0)
+    transpose_into(XT, XA, z * 256)
     gather_a(0)
-    transpose_into(XT, XA, z * 256)
     gather_a(1)
+    token_two()
     gather_b(0)
-    token_two()
     gather_a(2)
+    z_own(DOWN)
     gather_b(1)
-    z_own(DOWN)
     gather_c(0)
+    gather_b(2)
+    gather_a(3)
     cross_one()
-    gather_b(2)
-    attn_forward(1)
     gather_c(1)
-    gather_a(3)
     gather_a(4)
     gather_a(5)
+    attn_forward(1)
+    gather_b(3)
+    gather_c(2)
+    gather_b(4)
     cross_two()
-    gather_c(2)
-    gather_b(3)
     attn_forward(2)
-    gather_b(4)
     gather_b(5)
     gather_a(6)
     gather_a(7)
+    gather_c(3)
+    gather_c(4)
     cross_three()
-    gather_c(3)
+    gather_c(5)
     attn_forward(3)
-    gather_c(4)
     gather_a(8)
+    gather_b(6)
+    norm_one()
+    ffn_forward(1)
+    gather_b(7)
+    ffn_forward(0)
+    ffn_down(0)
+    ffn_down(1)
     cross_four()
-    gather_c(5)
-    norm_one()
-    ffn_forward(0)
-    gather_b(6)
-    ffn_down(0)
-    gather_b(7)
+    gather_b(8)
+    ffn_forward(2)
+    gather_c(6)
+    transpose_into(FLT, FL)
+    gather_c(7)
+    gather_c(8)
+    factor_start()
+    ffn_forward(3)
+    ffn_down(2)
     cross_five()
-    ffn_forward(1)
-    gather_b(8)
-    factor_start()
-    ffn_down(1)
-    ffn_forward(2)
-    transpose_into(FLT, FL)
-    gather_c(6)
-    ffn_forward(3)
-    gather_c(7)
-    ffn_down(2)
-    gather_c(8)
     ffn_down(3)
-    factor_two()
     norm_two()
     output_rows()
     loads["cot"].wait()
     norm_two_back()
     transpose_into(FDLT, FDL)
+    factor_two()
     ffn_back_one(3)
     grad_down(3)
     grad_up(3)
@@ -1154,15 +1156,11 @@
 
 
 def settle_kernel(*refs):
-    sources, targets, held, sems = refs[:9], refs[9:18], refs[18:27], refs[27]
-    arrive = [pltpu.make_async_copy(sources[i], held[i], sems.at[0, i]) for i in range(9)]
-    leave = [pltpu.make_async_copy(held[i], targets[i], sems.at[1, i]) for i in range(9)]
-    for copy in arrive:
+    sources, targets, sems = refs[:9], refs[9:18], refs[18]
+    copies = [pltpu.make_async_copy(sources[i], targets[i], sems.at[i]) for i in range(9)]
+    for copy in copies:
         copy.start()
-    for i in range(9):
-        arrive[i].wait()
-        leave[i].start()
-    for copy in leave:
+    for copy in copies:
         copy.wait()
 
 
@@ -1180,15 +1178,15 @@
     results = pl.pallas_call(
         fused_kernel,
         out_shape=(
-            jax.ShapeDtypeStruct((1, 256, 768), BF16),
-            jax.ShapeDtypeStruct((1, 256, 768), BF16),
-            jax.ShapeDtypeStruct((2, 3, BLK, 192), F32),
-            jax.ShapeDtypeStruct((2, 192, BLK), F32),
-            jax.ShapeDtypeStruct((2, BLK, 768), F32),
-            jax.ShapeDtypeStruct((2, BLK, 768), F32),
-            jax.ShapeDtypeStruct((2, BLK), F32),
-            jax.ShapeDtypeStruct((2, BLK), F32),
-            jax.ShapeDtypeStruct((2, 2, BLK), F32),
+            pltpu.VMEM((1, 256, 768), BF16),
+            pltpu.VMEM((1, 256, 768), BF16),
+            pltpu.VMEM((2, 3, BLK, 192), F32),
+            pltpu.VMEM((2, 192, BLK), F32),
+            pltpu.VMEM((2, BLK, 768), F32),
+            pltpu.VMEM((2, BLK, 768), F32),
+            pltpu.VMEM((2, BLK), F32),
+            pltpu.VMEM((2, BLK), F32),
+            pltpu.VMEM((2, 2, BLK), F32),
         ),
         in_specs=[whole, whole, whole, vmem, whole, whole, whole, whole, vmem, vmem],
         out_specs=(vmem,) * 9,
@@ -1236,8 +1234,8 @@
             sem((13,)),
             sem((12, 2)),
             sem((12,)),
-            sem((5, 9)),
-            sem((5, 9)),
+            sem((7, 9)),
+            sem((7, 9)),
             sem((9, 12)),
             sem((9, 12)),
             sem((7, 3)),
@@ -1248,7 +1246,7 @@
             sem((7,)),
         ],
         compiler_params=pltpu.CompilerParams(
-            collective_id=0, has_side_effects=True, vmem_limit_bytes=63 * 2**20
+            collective_id=0, has_side_effects=True, vmem_limit_bytes=59 * 2**20
         ),
     )(
         inputs, cotangent, cotangent.reshape(8, SEG, 768), doc_ids, wq, wo, wu, wd, norm_gain, norm_shift
@@ -1258,8 +1256,8 @@
         out_shape=tuple(jax.ShapeDtypeStruct(v.shape, v.dtype) for v in results),
         in_specs=[whole] * 9,
         out_specs=(whole,) * 9,
-        scratch_shapes=[pltpu.VMEM(v.shape, v.dtype) for v in results] + [sem((2, 9))],
-    )(*results)
+        scratch_shapes=[sem((9,))],
+    )(*[pltpu.with_memory_space_constraint(v, pltpu.VMEM) for v in results])
     return final[:5] + (final[5].swapaxes(1, 2),) + final[6:]
 
 

time: 135 us -> 130 us (0.963)
  Pallas kernels: 134 us -> 129 us
    pallas_call x1, Pallas kernels: 131 us -> 128 us  [fused_body(): pl.pallas_call(fused_kernel, out_shape=(pltpu.VMEM((1, 256, 768), BF16),...]
where the time goes in v5:
time: 130 us
  Pallas kernels  129 us (99%)
    pallas_call x1, Pallas kernels, fused_body(): pl.pallas_call(fused_kernel, out_shape=(pltpu.VMEM((1, 256, 768), BF16),...  128 us

profile of v5, /device:TPU:0, one launch (start us, length us, event | category | flops | bytes accessed | tf_op | source)
XLA Modules:
  0.0 130.0 jit_solution(8053709892029607455)
XLA Ops:
  0.6 127.6 %shard_map.160 = (bf16[1,256,768]{2,1,0:T(8,128)(2,1)S(1)}, bf16[1,256,768]{2,1,0:T(8,128)(2,1)S(1)}, f32[2,3,96,192]{3,2,1,0:T(8,128)S(1)}, f32[2,192,96]{2,1,0...) custom-call(bf16[1,1024,768]{2,1,0:T(8,128)(2,1)} %tokens_hbm.1, ...), custom_call_target="tpu_custom_call" | custom-call | tf_op jit(solution)/shard_map/pallas_call | solution.py:1178
  128.3 1.6 %shard_map.161 = (bf16[1,256,768]{2,1,0:T(8,128)(2,1)}, bf16[1,256,768]{2,1,0:T(8,128)(2,1)}, f32[2,3,96,192]{3,2,1,0:T(8,128)}, f32[2,192,96]{2,1,0:T(8,128)}, ...) custom-call(bf16[1,256,768]{2,1,0:T(8,128)(2,1)S(1)} %get-tuple-elem, ...), custom_call_target="tpu_custom_call" | custom-call | tf_op jit(solution)/shard_map/pallas_call | solution.py:1254

commit v6 on v5

--- a/solution.py
+++ b/solution.py
@@ -355,6 +355,12 @@
         sends.append(copy)
         return copy
 
+    barrier = pltpu.get_barrier_semaphore()
+    for m in range(1, 8):
+        pl.semaphore_signal(barrier, inc=1, device_id=(plane_index(m), z), device_id_type=MESH)
+    for r in range(1, 4):
+        pl.semaphore_signal(barrier, inc=1, device_id=z_peer[r], device_id_type=MESH)
+
     loads = {}
 
     def load(name, index, src, dst):
@@ -362,10 +368,10 @@
         copy.start()
         loads[name] = copy
 
-    load("x", 0, tokens_hbm.at[0], XA)
     load("wqk", 1, wq_hbm.at[0, pl.ds(0, 2)], W.at[ATT, z, 0])
     load("wv", 9, wq_hbm.at[0, 2], W.at[ATT, z, 1, 0])
     load("wo", 10, wo_hbm.at[0], W.at[ATT, z, 1, 1])
+    load("x", 0, tokens_hbm.at[0], XA)
     load("wu", 2, wu_hbm.at[0], W.at[UP, z])
     load("wd", 3, wd_hbm.at[0], W.at[DOWN, z])
     load("cot", 4, cot_hbm.at[0, pl.ds(pl.multiple_of(z * 256, 256), 256)], COT)
@@ -376,11 +382,6 @@
     load("l1d", 7, wd_hbm.at[1], L1.at[DOWN])
     load("c8", 8, cot_seg.at[:, pl.ds(0, 16)], C8)
 
-    barrier = pltpu.get_barrier_semaphore()
-    for m in range(1, 8):
-        pl.semaphore_signal(barrier, inc=1, device_id=(plane_index(m), z), device_id_type=MESH)
-    for r in range(1, 4):
-        pl.semaphore_signal(barrier, inc=1, device_id=z_peer[r], device_id_type=MESH)
     pl.semaphore_wait(barrier, 10)
 
     own_unit = [W.at[ATT, z], wu_hbm.at[0], wd_hbm.at[0]]
@@ -493,7 +494,7 @@
             MIX[r, rows, :] = jnp.concatenate(mixes, axis=-1).astype(BF16)
             return carry
 
-        lax.fori_loop(0, 2, segment, 0)
+        lax.fori_loop(0, 2, segment, 0, unroll=True)
         accumulate(r == 0, mm(MIX[r], out_rows(W.at[ATT, z_of[r]])))
 
     own_rows = pl.ds(pl.multiple_of(z * 256, 256), 256)
@@ -502,7 +503,7 @@
         def one(i, carry):
             return body(i, pl.ds(pl.multiple_of(i * 64, 64), 64), carry)
 
-        return lax.fori_loop(0, 4, one, init)
+        return lax.fori_loop(0, 4, one, init, unroll=True)
 
     g00, g01 = gain_ref[0, 0:1, :], gain_ref[0, 1:2, :]
     b00, b01 = shift_ref[0, 0:1, :], shift_ref[0, 1:2, :]
@@ -530,7 +531,7 @@
             DG[r, :, part] = slope.astype(DG.dtype)
             return carry
 
-        lax.fori_loop(0, 3, block, 0)
+        lax.fori_loop(0, 3, block, 0, unroll=True)
 
     def ffn_down(r):
         arrived(DOWN, r)
@@ -619,7 +620,7 @@
             g[jy, jx, c] = add_low(g[jy, jx, c], RC[i, jy, jx])
             return carry
 
-        lax.fori_loop(0, 4, block, 0)
+        lax.fori_loop(0, 4, block, 0, unroll=True)
         if k == ATT:
             part_a, part_b = g.at[:, nx, c, top], g.at[ny, :, c, low]
             peer_a, peer_b = x_peer, y_peer
@@ -717,7 +718,7 @@
             ref[:, :, :, :, part] = value.astype(BF16).reshape(2, 2, 2, BLK, 256)
             return carry
 
-        lax.fori_loop(0, 3, block, 0)
+        lax.fori_loop(0, 3, block, 0, unroll=True)
 
     def ffn_back_one(r):
         ga = mm_nt(FDL[...], cols(DOWN, r, 0, 768))
@@ -912,7 +913,7 @@
             GQ[rows, :] = jnp.concatenate(gqs + gks + gvs, axis=-1).astype(BF16)
             return carry
 
-        lax.fori_loop(0, 2, segment, 0)
+        lax.fori_loop(0, 2, segment, 0, unroll=True)
         store_unit(
             grad_unit(ATT, r),
             [
@@ -1042,8 +1043,8 @@
     gather_a(4)
     gather_a(5)
     attn_forward(1)
+    gather_c(2)
     gather_b(3)
-    gather_c(2)
     gather_b(4)
     cross_two()
     attn_forward(2)
@@ -1055,23 +1056,23 @@
     cross_three()
     gather_c(5)
     attn_forward(3)
+    gather_b(6)
     gather_a(8)
-    gather_b(6)
     norm_one()
+    ffn_forward(2)
+    gather_b(7)
     ffn_forward(1)
-    gather_b(7)
     ffn_forward(0)
     ffn_down(0)
-    ffn_down(1)
+    gather_c(6)
     cross_four()
     gather_b(8)
-    ffn_forward(2)
-    gather_c(6)
+    ffn_down(1)
     transpose_into(FLT, FL)
+    ffn_forward(3)
     gather_c(7)
     gather_c(8)
     factor_start()
-    ffn_forward(3)
     ffn_down(2)
     cross_five()
     ffn_down(3)
@@ -1081,72 +1082,72 @@
     norm_two_back()
     transpose_into(FDLT, FDL)
     factor_two()
+    grad_down(3)
     ffn_back_one(3)
-    grad_down(3)
     grad_up(3)
     ffn_back_two(3)
     ffn_back_one(2)
+    grad_down(2)
     sum_one(0)
-    grad_down(2)
+    grad_up(2)
     sum_one(1)
-    grad_up(2)
     ffn_back_two(2)
     ffn_back_one(1)
     sum_one(2)
     grad_down(1)
     sum_one(3)
     grad_up(1)
+    grad_down(0)
     sum_two(0)
     sum_z(0)
+    sum_one(4)
     ffn_back_two(1)
-    sum_one(4)
     ffn_back_one(0)
     sum_one(5)
-    grad_down(0)
+    sum_two(1)
+    sum_one(6)
+    sum_z(1)
     grad_up(0)
-    sum_two(1)
-    sum_z(1)
     ffn_back_two(0)
     turn_to_attention()
-    sum_one(6)
-    sum_one(7)
     sum_two(2)
     attn_backward(3)
     sum_two(3)
+    sum_one(7)
     sum_z(2)
     attn_backward(2)
     sum_two(4)
+    sum_one(8)
     sum_z(4)
-    sum_one(8)
     attn_backward(1)
+    sum_z(3)
+    sum_one(9)
     sum_two(5)
-    sum_z(3)
     sum_z(5)
+    sum_two(6)
     attn_backward(0)
-    sum_two(6)
+    sum_two(7)
     factor_three()
     ing_ref[0] = (GF[...] + ACC[...]).astype(BF16)
     norm_grads_two()
-    sum_two(7)
-    sum_one(9)
+    sum_two(8)
+    sum_one(10)
     factor_final()
-    sum_two(8)
+    sum_two(9)
     sum_z(6)
-    sum_one(10)
-    sum_two(9)
     sum_one(11)
     sum_three(8)
     sum_z(8)
-    write_unit(0, DOWN, sum_final(DOWN))
     sum_two(10)
     sum_three(9)
+    write_unit(0, DOWN, sum_final(DOWN))
     sum_z(9)
+    sum_two(11)
     sum_z(7)
-    sum_two(11)
     sum_three(10)
     sum_z(10)
+    sum_three(11)
     write_unit(0, UP, sum_final(UP))
-    sum_three(11)
     sum_z(11)
     norm_grads_final()
     write_unit(0, ATT, sum_final(ATT))

time: 130 us -> 127 us (0.977)
  Pallas kernels: 129 us -> 126 us
    pallas_call x1, Pallas kernels: 128 us -> 125 us  [fused_body(): pl.pallas_call(fused_kernel, out_shape=(pltpu.VMEM((1, 256, 768), BF16),...]
where the time goes in v6:
time: 127 us
  Pallas kernels  126 us (99%)
    pallas_call x1, Pallas kernels, fused_body(): pl.pallas_call(fused_kernel, out_shape=(pltpu.VMEM((1, 256, 768), BF16),...  125 us

profile of v6, /device:TPU:0, one launch (start us, length us, event | category | flops | bytes accessed | tf_op | source)
XLA Modules:
  0.0 127.0 jit_solution(2295062305565476461)
XLA Ops:
  0.6 124.5 %shard_map.160 = (bf16[1,256,768]{2,1,0:T(8,128)(2,1)S(1)}, bf16[1,256,768]{2,1,0:T(8,128)(2,1)S(1)}, f32[2,3,96,192]{3,2,1,0:T(8,128)S(1)}, f32[2,192,96]{2,1,0...) custom-call(bf16[1,1024,768]{2,1,0:T(8,128)(2,1)} %tokens_hbm.1, ...), custom_call_target="tpu_custom_call" | custom-call | tf_op jit(solution)/shard_map/pallas_call | solution.py:1179
  125.2 1.6 %shard_map.161 = (bf16[1,256,768]{2,1,0:T(8,128)(2,1)}, bf16[1,256,768]{2,1,0:T(8,128)(2,1)}, f32[2,3,96,192]{3,2,1,0:T(8,128)}, f32[2,192,96]{2,1,0:T(8,128)}, ...) custom-call(bf16[1,256,768]{2,1,0:T(8,128)(2,1)S(1)} %get-tuple-elem, ...), custom_call_target="tpu_custom_call" | custom-call | tf_op jit(solution)/shard_map/pallas_call | solution.py:1255

commit v7 on v6

--- a/solution.py
+++ b/solution.py
@@ -321,8 +321,8 @@
 def fused_kernel(
     tokens_hbm, cot_hbm, cot_seg, doc_ref, wq_hbm, wo_hbm, wu_hbm, wd_hbm, gain_ref, shift_ref,
     out_ref, ing_ref, qkvg_ref, outg_ref, upg_ref, downg_ref, gaing_ref, shiftg_ref, crossg_ref,
-    W, G, RC, RA1, RB1, RA2, RB2, RZ, RZF, RF, L1, XA, COT, QKV, PR, MIX, ACT, DG, GU, GQ, ACC, SC1, SC2, GF,
-    FL, FLT, FDL, FDLT, XT, GM, C8, INV1, INV2, FAC, LT, GS, E, NV, SV, RSV,
+    W, G, RC, RA1, RB1, RA2, RB2, RZ, RZF, RF, L1, XA, COT, QKV, PR, MIX, ACT, DG, GU, GQ, ACC, SC1, GF,
+    FL, FLT, FDL, FDLT, XT, GM, C8, INV1, FAC, LT, GS, E, NV, SV, RSV,
     sem_local, zg_s, zg_r, ag_s, ag_r, rs_s, rs_r, e_s, e_r, f_s, f_r, v_s, v_r,
 ):
     dp = lax.axis_index("dp")
@@ -538,49 +538,16 @@
         accumulate(r == 0, mm(ACT[r], cols(DOWN, r, 0, 768)))
 
     def norm_two():
+        loads["cot"].wait()
+
         def chunk(i, rows, carry):
+            gains, shifts = carry
             first = SC1[rows, :] * g00 + b00
             scaled, inverse = normalize(first + ACC[rows, :])
-            SC2[rows, :] = scaled
-            INV2[rows, :] = jnp.broadcast_to(inverse, (64, 128))
             out_ref[0, rows, :] = (scaled * g01 + b01).astype(BF16)
-            return carry
-
-        row_chunks(chunk)
-
-    def transpose_into(dst, src, start=0):
-        for i in range(2):
-            dst[:, i * 128 : i * 128 + 128] = src[pl.ds(pl.multiple_of(start + i * 128, 128), 128), :].T
-
-    exch = {}
-
-    def exchange(e, value):
-        E[e, 0] = value
-        for r in range(1, 4):
-            exch[e, r] = remote(E.at[e, 0], E.at[e, r], e_s.at[e, r - 1], e_r.at[e, r - 1], z_peer[r])
-
-    def exchange_wait(e):
-        for r in range(1, 4):
-            exch[e, r].wait_recv()
-
-    def exchange_sum(e):
-        exchange_wait(e)
-        return (E[e, 0] + E[e, 1]) + (E[e, 2] + E[e, 3])
-
-    row_of = lax.broadcasted_iota(jnp.int32, (8, 768), 0)
-    pair_of = row_of // 2
-
-    def own_row(value, j):
-        return jnp.sum(jnp.where(row_of == 2 * z + j, value, 0.0), axis=0, keepdims=True)
-
-
-    def norm_two_back():
-        def chunk(i, rows, carry):
-            gains, shifts = carry
             which = lax.broadcasted_iota(jnp.int32, (64, 768), 0) + i * 64
             grad = jnp.where(which % SEG == 0, GS[i // 2][0:1, :], COT[rows, :].astype(F32))
-            scaled = SC2[rows, :]
-            fed = normalize_back(grad, scaled, INV2[rows, 0:1], g01)
+            fed = normalize_back(grad, scaled, inverse, g01)
             GF[rows, :] = fed
             FDL[rows, :] = fed.astype(BF16)
             return (
@@ -592,6 +559,31 @@
         gains, shifts = row_chunks(chunk, (zero, zero))
         NV[1:2, :] = gains
         NV[3:4, :] = shifts
+
+    def transpose_into(dst, src, start=0):
+        for i in range(2):
+            dst[:, i * 128 : i * 128 + 128] = src[pl.ds(pl.multiple_of(start + i * 128, 128), 128), :].T
+
+    exch = {}
+
+    def exchange(e, value):
+        E[e, 0] = value
+        for r in range(1, 4):
+            exch[e, r] = remote(E.at[e, 0], E.at[e, r], e_s.at[e, r - 1], e_r.at[e, r - 1], z_peer[r])
+
+    def exchange_wait(e):
+        for r in range(1, 4):
+            exch[e, r].wait_recv()
+
+    def exchange_sum(e):
+        exchange_wait(e)
+        return (E[e, 0] + E[e, 1]) + (E[e, 2] + E[e, 3])
+
+    row_of = lax.broadcasted_iota(jnp.int32, (8, 768), 0)
+    pair_of = row_of // 2
+
+    def own_row(value, j):
+        return jnp.sum(jnp.where(row_of == 2 * z + j, value, 0.0), axis=0, keepdims=True)
 
     def grad_unit(k, r):
         return W.at[UP, r] if k == ATT else G.at[k - 1, r]
@@ -1078,8 +1070,6 @@
     ffn_down(3)
     norm_two()
     output_rows()
-    loads["cot"].wait()
-    norm_two_back()
     transpose_into(FDLT, FDL)
     factor_two()
     grad_down(3)
@@ -1215,7 +1205,6 @@
             pltpu.VMEM((256, 768), F32),
             pltpu.VMEM((256, 768), F32),
             pltpu.VMEM((256, 768), F32),
-            pltpu.VMEM((256, 768), F32),
             pltpu.VMEM((256, 768), BF16),
             pltpu.VMEM((768, 256), BF16),
             pltpu.VMEM((256, 768), BF16),
@@ -1223,7 +1212,6 @@
             pltpu.VMEM((768, 256), BF16),
             pltpu.VMEM((256, 192), BF16),
             pltpu.VMEM((8, 16, 768), BF16),
-            pltpu.VMEM((256, 128), F32),
             pltpu.VMEM((256, 128), F32),
             pltpu.VMEM((2, 2, 2, 64, 768), BF16),
             pltpu.VMEM((768, 256), BF16),

time: 127 us -> 127 us (level)
  no operation moved by 1% of the time
where the time goes in v7:
time: 127 us
  Pallas kernels  126 us (99%)
    pallas_call x1, Pallas kernels, fused_body(): pl.pallas_call(fused_kernel, out_shape=(pltpu.VMEM((1, 256, 768), BF16),...  124 us

profile of v7, /device:TPU:0, one launch (start us, length us, event | category | flops | bytes accessed | tf_op | source)
XLA Modules:
  0.0 126.9 jit_solution(5975297853479898469)
XLA Ops:
  0.6 124.4 %shard_map.160 = (bf16[1,256,768]{2,1,0:T(8,128)(2,1)S(1)}, bf16[1,256,768]{2,1,0:T(8,128)(2,1)S(1)}, f32[2,3,96,192]{3,2,1,0:T(8,128)S(1)}, f32[2,192,96]{2,1,0...) custom-call(bf16[1,1024,768]{2,1,0:T(8,128)(2,1)} %tokens_hbm.1, ...), custom_call_target="tpu_custom_call" | custom-call | tf_op jit(solution)/shard_map/pallas_call | solution.py:1169
  125.1 1.6 %shard_map.161 = (bf16[1,256,768]{2,1,0:T(8,128)(2,1)}, bf16[1,256,768]{2,1,0:T(8,128)(2,1)}, f32[2,3,96,192]{3,2,1,0:T(8,128)}, f32[2,192,96]{2,1,0:T(8,128)}, ...) custom-call(bf16[1,256,768]{2,1,0:T(8,128)(2,1)S(1)} %get-tuple-elem, ...), custom_call_target="tpu_custom_call" | custom-call | tf_op jit(solution)/shard_map/pallas_call | solution.py:1243

commit v8 on v7

--- a/solution.py
+++ b/solution.py
@@ -1011,6 +1011,12 @@
             @pl.when(condition)
             def _(copy=copy):
                 copy.wait_send()
+
+    def settle_sends(keep):
+        for copy in sends[: len(sends) - keep]:
+            if id(copy) not in waited:
+                copy.wait_send()
+                waited.append(id(copy))
 
     for name in ("wqk", "wv", "wo"):
         loads[name].wait()
@@ -1136,6 +1142,7 @@
     sum_z(7)
     sum_three(10)
     sum_z(10)
+    settle_sends(8)
     sum_three(11)
     write_unit(0, UP, sum_final(UP))
     sum_z(11)

time: 127 us -> 127 us (level)
  no operation moved by 1% of the time
where the time goes in v8:
time: 127 us
  Pallas kernels  126 us (99%)
    pallas_call x1, Pallas kernels, fused_body(): pl.pallas_call(fused_kernel, out_shape=(pltpu.VMEM((1, 256, 768), BF16),...  124 us

profile of v8, /device:TPU:0, one launch (start us, length us, event | category | flops | bytes accessed | tf_op | source)
XLA Modules:
  0.0 126.7 jit_solution(16764658696956677861)
XLA Ops:
  0.6 124.3 %shard_map.160 = (bf16[1,256,768]{2,1,0:T(8,128)(2,1)S(1)}, bf16[1,256,768]{2,1,0:T(8,128)(2,1)S(1)}, f32[2,3,96,192]{3,2,1,0:T(8,128)S(1)}, f32[2,192,96]{2,1,0...) custom-call(bf16[1,1024,768]{2,1,0:T(8,128)(2,1)} %tokens_hbm.1, ...), custom_call_target="tpu_custom_call" | custom-call | tf_op jit(solution)/shard_map/pallas_call | solution.py:1176
  124.9 1.6 %shard_map.161 = (bf16[1,256,768]{2,1,0:T(8,128)(2,1)}, bf16[1,256,768]{2,1,0:T(8,128)(2,1)}, f32[2,3,96,192]{3,2,1,0:T(8,128)}, f32[2,192,96]{2,1,0:T(8,128)}, ...) custom-call(bf16[1,256,768]{2,1,0:T(8,128)(2,1)S(1)} %get-tuple-elem, ...), custom_call_target="tpu_custom_call" | custom-call | tf_op jit(solution)/shard_map/pallas_call | solution.py:1250
